TPU v7x, 512 devices: a whole 4x4x16 slice. The times are simulated.
512 devices in a mesh: dp: 64 (over z, y_lo, core), own: 8 (over y_hi, x).
Axes of the slice: x: 4, y: 4 (y_hi: 2, y_lo: 2; y = y_hi * 2 + y_lo), z: 16, core: 2. Of those that a mesh axis runs over, the one named last changes fastest.
Arguments:
- activations: bfloat16 [32768, 1, 1024], P('dp', None, 'own'), may hold values from -16 to 16
- output_grads: bfloat16 [32768, 3, 1024], P('dp', None, 'own'), may hold values from -16 to 16
- old_factors: float32 [4, 1024, 1024], P(None, 'dp', 'own'), may hold values from -2 to 2
- inverses: bfloat16 [8, 1, 1024, 1024], P('own', None, 'dp'), may hold values from -0.5 to 2.5, as said below
- owners: int32 [4], replicated, may hold values from 0 to 7, as said below
Outputs:
- new_factors: float32 [4, 1024, 1024], P(None, 'dp', 'own')
- preconditioned: float32 [3, 1024, 1, 1024], P(None, 'dp', None, 'own')
Inputs may be any that keep to these rules, and one draw needn't show every extreme that they name: `owners`: no owner is named by more than 1 block, and one owner by exactly 1. `inverses`: slot s of owner o holds the symmetric inverse block of the s-th block, in block order, that owners maps to o; slots that no block maps to are not read.
All inputs are finite; a program needn't handle non-finite values.
Results may differ from a plain program's by a relative error of at most 0.0013.
The roundings to bfloat16 on the way count: a program that leaves them out, or rounds other values in their place, can miss the bound.
Values may be sent and summed in bfloat16 or wider, within the bound.
A program may use at most 64 MiB of HBM per device.

v0:
```python
import jax
import jax.numpy as jnp
from jax import lax
from jax.sharding import PartitionSpec as P

FACTOR_DECAY = 0.9


def body(activations, output_grads, old_factors, inverses, owners):
    owner_count = lax.axis_size("own")
    dp_count = lax.axis_size("dp")
    my_owner = lax.axis_index("own")
    shard_cols = jnp.concatenate([activations, output_grads], axis=1)
    block_count = shard_cols.shape[1]
    act_count = activations.shape[1]
    slot_count = inverses.shape[1]
    total_tokens = shard_cols.shape[0] * dp_count
    gathered = lax.all_gather(shard_cols, "own", axis=2, tiled=True)
    partial_value = jnp.einsum(
        "tnr,tnc->nrc", gathered, shard_cols, preferred_element_type=jnp.float32
    )
    summed = lax.psum_scatter(partial_value, "dp", scatter_dimension=1, tiled=True)
    new_factors = FACTOR_DECAY * old_factors + (1.0 - FACTOR_DECAY) / total_tokens * summed
    positions = jnp.arange(block_count, dtype=jnp.int32)
    same_owner = owners[:, None] == owners[None, :]
    block_rank = jnp.sum(
        (same_owner & (positions[None, :] < positions[:, None])).astype(jnp.int32), axis=1
    )
    flat_slot = owners * slot_count + block_rank
    slot_positions = jnp.arange(owner_count * slot_count, dtype=jnp.int32)
    picker = (flat_slot[:, None] == slot_positions[None, :]).astype(jnp.bfloat16)
    rows_full = lax.all_gather(inverses, "dp", axis=2, tiled=True)[0]
    slot_ids = jnp.arange(slot_count, dtype=jnp.int32)
    my_slots = (owners[None, :] == my_owner) & (block_rank[None, :] == slot_ids[:, None])
    selector = my_slots.astype(jnp.bfloat16)
    chosen = jnp.einsum(
        "sn,tnk->stk", selector, gathered, preferred_element_type=jnp.float32
    ).astype(jnp.bfloat16)
    product = jnp.einsum(
        "stk,skj->stj", chosen, rows_full, preferred_element_type=jnp.float32
    ).astype(jnp.bfloat16)
    received = lax.all_to_all(product, "own", split_axis=2, concat_axis=0, tiled=True)
    scaled_cols = jnp.einsum(
        "nq,qtc->tnc", picker, received, preferred_element_type=jnp.float32
    ).astype(jnp.bfloat16)
    act_cols = scaled_cols[:, :act_count, :]
    grad_cols = scaled_cols[:, act_count:, :]
    gradient_term = jnp.einsum(
        "uoi,uns->oins",
        lax.all_gather(grad_cols, "own", axis=2, tiled=True),
        act_cols,
        preferred_element_type=jnp.float32,
    )
    preconditioned = (
        lax.psum_scatter(gradient_term, "dp", scatter_dimension=1, tiled=True) / total_tokens
    )
    return (new_factors, preconditioned)


def solution(mesh):
    placed = (
        P("dp", None, "own"),
        P("dp", None, "own"),
        P(None, "dp", "own"),
        P("own", None, "dp", None),
        P(),
    )
    return jax.shard_map(
        body,
        mesh=mesh,
        in_specs=placed,
        out_specs=(P(None, "dp", "own"), P(None, "dp", None, "own")),
        check_vma=False,
    )
```

profile of v0, /device:TPU:6, one launch (start us, length us, event | category | flops | bytes accessed | tf_op | source)
XLA Modules:
  0.0 844.1 jit_solution(14805443892643101670)
XLA Ops:
  7.2 0.0 all-gather.4.cloned.1.call-start
  7.2 0.9 constant_dynamic-update-slice_fusion.1
  8.1 1.0 constant_dynamic-update-slice_fusion
  9.2 0.8 copy-done
  10.0 0.0 all-gather.6.cloned.1.call-start
  10.1 0.7 all-gather.6.cloned.1.call-update
  10.8 0.9 convert_reduce_fusion
  11.7 97.1 %all-gather.4.cloned.1.call-done = bf16[512,4,1024]{2,0,1:T(8,128)(2,1)} async-done(((bf16[512,4,128]{2,0,1:T(8,128)(2,1)}), bf16[512,4,1024]{2,0,1:T(8,128)(2,1)}) %all-gather.4.cloned.1.call-update) | async-done | bytes 4194320 | tf_op jit(solution)/shard_map/all_gather | solution.py:18
  108.8 5.5 fusion
  114.3 117.9 %all-gather.6.cloned.1.call-done = bf16[1,1,1024,1024]{3,2,1,0:T(8,128)(2,1)} async-done(((bf16[1,1,16,1024]{3,2,1,0:T(8,128)(2,1)}), bf16[1,1,1024,1024]{3,2,1,0:T(8,128)(2,1)}) %all-gather.6.cloned.1.call-update) | async-done | bytes 2097168 | tf_op jit(solution)/shard_map/all_gather | solution.py:32
  232.3 2.8 fusion.12
  235.1 2.0 copy.19
  237.1 0.5 broadcast.14
  237.7 7.0 reduce
  244.7 1.6 reshape.34
  246.3 7.0 all-to-all-start
  253.3 14.9 %all-to-all-done = bf16[8,2,32768]{2,1,0:T(2,128)(2,1)S(1)} async-done(((bf16[8,2,32768]{2,1,0:T(2,128)(2,1)}), bf16[8,2,32768]{2,1,0:T(2,128)(2,1)S(1)}, u32[]{:S(2)}, u32[]{:S(2)}) %all-to-all-start) | async-done | bytes 1048608 | tf_op jit(solution)/shard_map/all_to_all | solution.py:42
  268.2 1.0 reshape.35
  269.2 0.3 copy.27
  269.5 0.8 copy.26
  270.3 0.5 fusion.15
  270.8 1.1 slice.8
  271.9 0.0 reduce-scatter.3.cloned.1.call-start
  272.0 5.2 fusion.28
  277.2 0.3 reduce-scatter.5.cloned.1.call-start
  277.4 0.2 slice.9
  277.6 100.5 %all-gather.8.cloned.1.call-done = bf16[512,3,1024]{2,1,0:T(4,128)(2,1)} async-done(((bf16[512,3,128]{2,1,0:T(4,128)(2,1)}), bf16[512,3,1024]{2,1,0:T(4,128)(2,1)}) %all-gather.8.cloned.1.call-update) | async-done | bytes 3145744 | tf_op jit(solution)/shard_map/all_gather | solution.py:50
  378.1 6.6 fusion.9
  384.8 223.6 %reduce-scatter.3.cloned.1.call-done = f32[4,16,128]{2,1,0:T(8,128)} async-done(((f32[4,1024,128]{2,1,0:T(8,128)}), f32[4,16,128]{2,1,0:T(8,128)}) %reduce-scatter.3.cloned.1.call-update) | async-done | bytes 32784 | tf_op jit(solution)/shard_map/reduce_scatter | solution.py:22
  608.4 1.4 multiply_add_fusion
  609.8 226.5 %reduce-scatter.5.cloned.1.call-done = f32[3,16,1,128]{3,1,0,2:T(8,128)} async-done(((f32[3,1024,1,128]{3,1,0,2:T(8,128)}), f32[3,16,1,128]{3,1,0,2:T(8,128)}) %reduce-scatter.5.cloned.1.call-update) | async-done | bytes 24592 | tf_op jit(solution)/shard_map/reduce_scatter | solution.py:55
  836.2 1.3 broadcast_multiply_fusion
  (13 shorter events, 0.1 us)
Async XLA Ops:
  7.2 101.6 %all-gather.4.cloned.1.call-start = ((), (), s32[]{:S(2)}) async-start(), calls=%async_computation.3 | async-start | bytes 4718592 | tf_op jit(solution)/shard_map/all_gather | solution.py:18
  9.2 0.8 copy-start
  10.0 222.2 %all-gather.6.cloned.1.call-start = ((), (), s32[]{:S(2)}) async-start(), calls=%async_computation.5 | async-start | bytes 2129920 | tf_op jit(solution)/shard_map/all_gather | solution.py:32
  244.7 8.6 %copy-start.3 = (s32[4]{0:T(128)S(1)}, s32[4]{0:T(128)}, u32[]{:S(2)}) copy-start(s32[4]{0:T(128)} %param.9) | copy-start | bytes 52
  246.3 21.9 %all-to-all-start = ((bf16[8,2,32768]{2,1,0:T(2,128)(2,1)}), bf16[8,2,32768]{2,1,0:T(2,128)(2,1)S(1)}, u32[]{:S(2)}, u32[]{:S(2)}) async-start(bf16[8,2,32768]{2,1,0:T(2,128)(2,1)} %reshape.34), calls=%async_computation.1 | async-start | bytes 2097152 | tf_op jit(solution)/shard_map/all_to_all | solution.py:42
  253.3 124.9 %all-gather.8.cloned.1.call-start = ((), (), s32[]{:S(2)}) async-start(), calls=%async_computation.6 | async-start | bytes 4718592 | tf_op jit(solution)/shard_map/all_gather | solution.py:50
  270.3 1.7 copy-start.1
  271.9 336.5 %reduce-scatter.3.cloned.1.call-start = ((), (), s32[]{:S(2)}) async-start(), calls=%async_computation.4 | async-start | bytes 2129920 | tf_op jit(solution)/shard_map/reduce_scatter | solution.py:22
  277.2 559.1 %reduce-scatter.5.cloned.1.call-start = ((), (), s32[]{:S(2)}) async-start(), calls=%async_computation.7 | async-start | bytes 1597440 | tf_op jit(solution)/shard_map/reduce_scatter | solution.py:55
  277.6 330.8 %copy-start.2 = (f32[4,16,128]{2,1,0:T(8,128)S(1)}, f32[4,16,128]{2,1,0:T(8,128)}, u32[]{:S(2)}) copy-start(f32[4,16,128]{2,1,0:T(8,128)} %param.7) | copy-start | bytes 98308
Sparse Core Ops, SparseCore 0:
  11.1 97.6 all-gather.3
  110.9 121.2 all-gather.5
  272.0 106.0 all-gather.7
  380.8 227.5 reduce-scatter.2
  611.2 224.9 reduce-scatter.4
where the time goes:
time: 845 us; the launch traced here: 844 us
  waiting for transfers between devices  781 us (92%)
  matrix products  20.6 us (2%)
  between operations  13.9 us (2%)
  other arithmetic  10.7 us (1%)
  local copies, waits for them, and re-layouts  10.3 us (1%)
    reduce_scatter x1, waiting for transfers between devices, body(): lax.psum_scatter(gradient_term, 'dp', scatter_dimension=1, tiled=True)  226 us
    reduce_scatter x1, waiting for transfers between devices, body(): lax.psum_scatter(partial_value, 'dp', scatter_dimension=1, tiled=True)  224 us
    all_gather x1, waiting for transfers between devices, body(): rows_full = lax.all_gather(inverses, 'dp', axis=2, tiled=True)[0]  118 us
    all_gather x1, waiting for transfers between devices, body(): lax.all_gather(grad_cols, 'own', axis=2, tiled=True)  101 us
    all_gather x1, waiting for transfers between devices, body(): gathered = lax.all_gather(shard_cols, 'own', axis=2, tiled=True)  97.1 us
  transfers between devices with their start and end apart: 6, of which 6 were waited for; matrix products, arithmetic and copies ran while one was open for 2% of the time, Pallas kernels for 0%

commit v1 on v0

v1 whole, which is shorter than its diff:
```python
import functools

import jax
import jax.numpy as jnp
from jax import lax
from jax.experimental import pallas as pl
from jax.experimental.pallas import tpu as pltpu
from jax.sharding import PartitionSpec as P

MESH = pl.DeviceIdType.MESH
FACTOR_DECAY = 0.9
TOKENS = 32768
TOK = 512
NZ = 16
HALF = NZ // 2
PIECES = 4
Q = 2
PER = PIECES // Q
LANE = 128
ROWS = 16


def gram(lhs8, rhs4, part, j_base):
    rhs = jnp.concatenate([rhs4[j_base + j] for j in range(PIECES)], axis=1)

    def tile(i, _):
        lhs = jnp.concatenate([lhs8[2 * i], lhs8[2 * i + 1]], axis=1)
        out = lax.dot_general(lhs, rhs, (((0,), (0,)), ((), ())), preferred_element_type=jnp.float32)
        for j in range(PIECES):
            part[j, pl.ds(4 * i, 4)] = out[:, j * LANE:(j + 1) * LANE].reshape(4, 2, 2, ROWS, LANE)
        return 0

    lax.fori_loop(0, 4, tile, 0)


def kernel(
    act, grads, old, inv, owners, nf_out, pr_out,
    cols, x8, shard, full_inv, s8, a4,
    part_c, part_p, half_c, half_p, right_c, right_p, left_c, left_p,
    ysum_c, ysum_p, yrecv_c, yrecv_p, fin_c, fin_p, frecv_c, frecv_p,
    loc_sem, xs_sem, xr_sem, is_sem, ir_sem, ns_sem, nr_sem, gs_sem, gr_sem,
    ss_sem, sr_sem, as_sem, ar_sem, cs_sem, cr_sem, rs_sem, rr_sem, ls_sem, lr_sem,
    ys_sem, yr_sem, fs_sem, fr_sem,
):
    dp = lax.axis_index("dp")
    own = lax.axis_index("own")
    z = dp // 4
    y = (dp // 2) % 2
    c = dp % 2
    h = own // 4
    x = own % 4

    def at(zz, yy, cc):
        return ((zz * 2 + yy) * 2 + cc, own)

    def member(hh, xx):
        return (dp, hh * 4 + xx)

    up = at((z + 1) % NZ, y, c)
    down = at((z + NZ - 1) % NZ, y, c)
    core = at(z, y, 1 - c)
    across = at(z, 1 - y, c)
    diagonal = at(z, 1 - y, 1 - c)
    peers = [((h + d // 4) % 2, (x + d % 4) % 4) for d in range(8)]

    loc = [
        pltpu.make_async_copy(act, cols.at[pl.ds(0, 1)], loc_sem.at[0]),
        pltpu.make_async_copy(grads, cols.at[pl.ds(1, 3)], loc_sem.at[1]),
        pltpu.make_async_copy(inv.at[:, pl.ds(h * 512, 512)], shard.at[own], loc_sem.at[2]),
    ]
    for copy in loc:
        copy.start()

    barrier = pltpu.get_barrier_semaphore()
    targets = [member(*peers[d]) for d in range(1, 8)] + [up, down, core, across, diagonal]
    for target in targets:
        pl.semaphore_signal(barrier, inc=1, device_id=target, device_id_type=MESH)
    pl.semaphore_wait(barrier, len(targets))

    sends = []

    def send(src, dst, s_sem, r_sem, target):
        copy = pltpu.make_async_remote_copy(
            src_ref=src, dst_ref=dst, send_sem=s_sem, recv_sem=r_sem, device_id=target, device_id_type=MESH
        )
        copy.start()
        return copy

    inv_copies = []
    for d in range(1, 8):
        hh, xx = peers[d]
        inv_copies.append(
            send(inv.at[:, pl.ds(hh * 512, 512)], shard.at[own], is_sem.at[d], ir_sem.at[d], member(hh, xx))
        )
    loc[0].wait()
    loc[1].wait()
    x_copies = []
    for d in range(1, 8):
        hh, xx = peers[d]
        x_copies.append(send(cols.at[xx], x8.at[own], xs_sem.at[d], xr_sem.at[d], member(hh, xx)))
    x8[own] = cols[x]
    loc[2].wait()

    for copy in inv_copies:
        copy.wait_recv()
    full_inv[dp] = shard[owners[x]]
    near = [
        send(full_inv.at[dp], full_inv.at[dp], ns_sem.at[k], nr_sem.at[k], target)
        for k, target in enumerate((core, across, diagonal))
    ]
    for copy in near:
        copy.wait_recv()

    def block(zz):
        return full_inv.at[pl.ds(((zz + NZ) % NZ) * 4, 4)]

    def gather_copy(s, right):
        zz = z - s if right else z + s
        k = s if right else HALF + s
        return pltpu.make_async_remote_copy(
            src_ref=block(zz), dst_ref=block(zz), send_sem=gs_sem.at[k], recv_sem=gr_sem.at[k],
            device_id=up if right else down, device_id_type=MESH,
        )

    for s in range(HALF):
        if s > 0:
            gather_copy(s - 1, True).wait_recv()
        gather_copy(s, True).start()
        if s < HALF - 1:
            if s > 0:
                gather_copy(s - 1, False).wait_recv()
            gather_copy(s, False).start()

    for copy in x_copies:
        copy.wait_recv()
    gram(x8, x8, part_c, h * PIECES)

    def order(k):
        if k == 15:
            return z
        return (z + HALF - k // 2) % NZ if k % 2 == 0 else (z + NZ - HALF + 1 + k // 2) % NZ

    def core_copy(n, part, half, k):
        t = order(k)
        return pltpu.make_async_remote_copy(
            src_ref=part.at[:, t, :, 1 - c], dst_ref=half.at[:, t],
            send_sem=cs_sem.at[n, k], recv_sem=cr_sem.at[n, k], device_id=core, device_id_type=MESH,
        )

    for k in range(16):
        core_copy(0, part_c, half_c, k).start()

    gather_copy(HALF - 1, True).wait_recv()
    gather_copy(HALF - 2, False).wait_recv()

    weights = full_inv[...].reshape(1024, 512)

    def scale_tile(i, _):
        rows = pl.ds(pl.multiple_of(i * 256, 256), 256)
        lhs = jnp.concatenate([x8[k, rows, :] for k in range(8)], axis=1)
        out = jnp.dot(lhs, weights, preferred_element_type=jnp.float32).astype(jnp.bfloat16)
        for j in range(PIECES):
            s8[h * PIECES + j, rows, :] = out[:, j * LANE:(j + 1) * LANE]
        return 0

    lax.fori_loop(0, TOK // 256, scale_tile, 0)

    mine = s8.at[pl.ds(h * PIECES, PIECES)]
    theirs = s8.at[pl.ds((1 - h) * PIECES, PIECES)]

    def swap_copy():
        return pltpu.make_async_remote_copy(
            src_ref=mine, dst_ref=mine, send_sem=ss_sem.at[0], recv_sem=sr_sem.at[0],
            device_id=member(1 - h, x), device_id_type=MESH,
        )

    def act_copy(g):
        return pltpu.make_async_remote_copy(
            src_ref=mine, dst_ref=a4, send_sem=as_sem.at[g], recv_sem=ar_sem.at[0],
            device_id=member(h, g), device_id_type=MESH,
        )

    @pl.when(x == 0)
    def _():
        for g in (1, 2, 3):
            act_copy(g).start()

    @pl.when(x > 0)
    def _():
        swap_copy().start()

    def reduce_scatter(n, part, half, right, left, ysum, yrecv, fin):
        def own_rows(t, js):
            return part[js, t, :, c] + half[js, t]

        def ring_copy(s, q, is_right):
            buf = right if is_right else left
            sem, rsem = (rs_sem, rr_sem) if is_right else (ls_sem, lr_sem)
            js = pl.ds(q * PER, PER)
            return pltpu.make_async_remote_copy(
                src_ref=buf.at[s, js], dst_ref=buf.at[s + 1, js],
                send_sem=sem.at[n, s, q], recv_sem=rsem.at[n, s, q],
                device_id=up if is_right else down, device_id_type=MESH,
            )

        for s in range(HALF):
            for is_right in (True, False):
                if not is_right and s == HALF - 1:
                    continue
                k = 2 * s if is_right else 2 * s + 1
                buf = right if is_right else left
                core_copy(n, part, half, k).wait_recv()
                for q in range(Q):
                    js = pl.ds(q * PER, PER)
                    term = own_rows(order(k), js)
                    if s > 0:
                        ring_copy(s - 1, q, is_right).wait_recv()
                        term = term + buf[s, js]
                    buf[s, js] = term
                    ring_copy(s, q, is_right).start()
        core_copy(n, part, half, 15).wait_recv()
        for q in range(Q):
            js = pl.ds(q * PER, PER)
            ring_copy(HALF - 1, q, True).wait_recv()
            ring_copy(HALF - 2, q, False).wait_recv()
            ysum[js] = own_rows(z, js) + right[HALF, js] + left[HALF - 1, js]
        cross = pltpu.make_async_remote_copy(
            src_ref=ysum.at[:, 1 - y], dst_ref=yrecv, send_sem=ys_sem.at[n], recv_sem=yr_sem.at[n],
            device_id=across, device_id_type=MESH,
        )
        cross.start()
        cross.wait_recv()
        fin[...] = ysum[:, y] + yrecv[...]
        for k in range(16):
            core_copy(n, part, half, k).wait_send()
        for s in range(HALF):
            for q in range(Q):
                ring_copy(s, q, True).wait_send()
                if s < HALF - 1:
                    ring_copy(s, q, False).wait_send()
        cross.wait_send()

    def final_copy(n, d, fin, frecv):
        xx = (x + d) % 4
        return pltpu.make_async_remote_copy(
            src_ref=fin.at[xx], dst_ref=frecv.at[x], send_sem=fs_sem.at[n, d], recv_sem=fr_sem.at[n, d],
            device_id=member(h, xx), device_id_type=MESH,
        )

    reduce_scatter(0, part_c, half_c, right_c, left_c, ysum_c, yrecv_c, fin_c)
    for d in (1, 2, 3):
        final_copy(0, d, fin_c, frecv_c).start()
    frecv_c[x] = fin_c[x]

    @pl.when(x == 0)
    def _():
        for g in (1, 2, 3):
            act_copy(g).wait_send()

    @pl.when(x > 0)
    def _():
        act_copy(0).wait_recv()
        swap_copy().wait_recv()
        gram(s8, a4, part_p, 0)
        for k in range(16):
            core_copy(1, part_p, half_p, k).start()
        reduce_scatter(1, part_p, half_p, right_p, left_p, ysum_p, yrecv_p, fin_p)
        for d in (1, 2, 3):
            final_copy(1, d, fin_p, frecv_p).start()
        frecv_p[x] = fin_p[x]
        swap_copy().wait_send()

    for d in (1, 2, 3):
        final_copy(0, d, fin_c, frecv_c).wait_recv()
    nf_out[...] = FACTOR_DECAY * old[...] + ((1.0 - FACTOR_DECAY) / TOKENS) * frecv_c[...]

    for d in (1, 2, 3):
        @pl.when((x + 4 - d) % 4 > 0)
        def _():
            final_copy(1, d, fin_p, frecv_p).wait_recv()
    pr_out[...] = frecv_p[1:4] * (1.0 / TOKENS)

    for copy in inv_copies + x_copies + near:
        copy.wait_send()
    for s in range(HALF):
        gather_copy(s, True).wait_send()
        if s < HALF - 1:
            gather_copy(s, False).wait_send()
    for d in (1, 2, 3):
        final_copy(0, d, fin_c, frecv_c).wait_send()

    @pl.when(x > 0)
    def _():
        for d in (1, 2, 3):
            final_copy(1, d, fin_p, frecv_p).wait_send()


def body(activations, output_grads, old_factors, inverses, owners):
    vmem = pl.BlockSpec(memory_space=pltpu.VMEM)
    hbm = pl.BlockSpec(memory_space=pl.ANY)
    bf16, f32 = jnp.bfloat16, jnp.float32
    twice = lambda shape: [pltpu.VMEM(shape, f32)] * 2
    dma = lambda *shape: pltpu.SemaphoreType.DMA(shape)
    new_factors, preconditioned = pl.pallas_call(
        kernel,
        out_shape=(
            jax.ShapeDtypeStruct((4, ROWS, LANE), f32),
            jax.ShapeDtypeStruct((3, ROWS, LANE), f32),
        ),
        in_specs=[hbm, hbm, vmem, hbm, pl.BlockSpec(memory_space=pltpu.SMEM)],
        out_specs=(vmem, vmem),
        scratch_shapes=[
            pltpu.VMEM((4, TOK, LANE), bf16),
            pltpu.VMEM((8, TOK, LANE), bf16),
            pltpu.VMEM((8, ROWS, 512), bf16),
            pltpu.VMEM((64, ROWS, 512), bf16),
            pltpu.VMEM((8, TOK, LANE), bf16),
            pltpu.VMEM((4, TOK, LANE), bf16),
            *twice((PIECES, NZ, 2, 2, ROWS, LANE)),
            *twice((PIECES, NZ, 2, ROWS, LANE)),
            *twice((HALF + 1, PIECES, 2, ROWS, LANE)),
            *twice((HALF, PIECES, 2, ROWS, LANE)),
            *twice((PIECES, 2, ROWS, LANE)),
            *twice((PIECES, ROWS, LANE)),
            *twice((PIECES, ROWS, LANE)),
            *twice((PIECES, ROWS, LANE)),
            dma(3),
            dma(8), dma(8), dma(8), dma(8), dma(3), dma(3), dma(16), dma(16),
            dma(1), dma(1), dma(4), dma(1), dma(2, 16), dma(2, 16),
            dma(2, HALF, Q), dma(2, HALF, Q), dma(2, HALF, Q), dma(2, HALF, Q),
            dma(2), dma(2), dma(2, 4), dma(2, 4),
        ],
        compiler_params=pltpu.CompilerParams(
            collective_id=0, has_side_effects=True, vmem_limit_bytes=40 * 1024 * 1024
        ),
    )(
        jnp.swapaxes(activations, 0, 1),
        jnp.swapaxes(output_grads, 0, 1),
        old_factors,
        inverses.reshape(ROWS, 1024),
        owners,
    )
    return new_factors, preconditioned.reshape(3, ROWS, 1, LANE)


def solution(mesh):
    placed = (
        P("dp", None, "own"),
        P("dp", None, "own"),
        P(None, "dp", "own"),
        P("own", None, "dp", None),
        P(),
    )
    return jax.shard_map(
        body,
        mesh=mesh,
        in_specs=placed,
        out_specs=(P(None, "dp", "own"), P(None, "dp", None, "own")),
        check_vma=False,
    )
```

time: 845 us -> 132 us (0.16)
  waiting for transfers between devices: 781 us -> 0 us
  Pallas kernels: 0 us -> 126 us
  matrix products: 20.6 us -> 0 us
  between operations: 13.9 us -> 0.65 us
  other arithmetic: 10.7 us -> 0 us
    reduce_scatter x2 -> x0, waiting for transfers between devices: 450 us -> none  [the longest x1 226 us: body(): lax.psum_scatter(gradient_term, 'dp', scatter_dimension=1, tiled=True)]
    all_gather x3 -> x0, waiting for transfers between devices: 316 us -> none  [the longest x1 118 us: body(): rows_full = lax.all_gather(inverses, 'dp', axis=2, tiled=True)[0]]
    pallas_call x0 -> x1, Pallas kernels: none -> 126 us  [body(): pl.pallas_call(kernel, out_shape=(jax.ShapeDtypeStruct((4, ROWS, LANE), f...]
    dot_general x5 -> x0, matrix products: 20.6 us -> none  [the longest x1 6.62 us: body(): jnp.einsum('uoi,uns->oins', lax.all_gather(grad_cols, 'own', axis=2, tile...]
    all_to_all x1 -> x0, waiting for transfers between devices: 14.9 us -> none  [body(): lax.all_to_all(product, 'own', split_axis=2, concat_axis=0, tiled=True)]
  transfers between devices with their start and end apart: 6 -> 0, of which waited for: 6 -> 0; matrix products, arithmetic and copies ran while one was open for 2% -> 0% of each run, Pallas kernels for 0% -> 0%
where the time goes in v1:
time: 132 us
  Pallas kernels  126 us (95%)
  local copies, waits for them, and re-layouts  5.29 us (4%)
    pallas_call x1, Pallas kernels, body(): pl.pallas_call(kernel, out_shape=(jax.ShapeDtypeStruct((4, ROWS, LANE), f...  126 us
    unnamed x12, local copies, waits for them, and re-layouts  5.29 us

profile of v1, /device:TPU:6, one launch (start us, length us, event | category | flops | bytes accessed | tf_op | source)
XLA Modules:
  0.0 131.6 jit_solution(5361706170387437985)
XLA Ops:
  0.6 0.0 copy-start.4
  0.6 0.6 copy-done.4
  1.3 0.0 copy-start
  1.3 1.0 copy-done
  2.3 0.0 copy-start.1
  2.3 0.9 copy-done.1
  3.2 0.0 copy-start.2
  3.2 0.8 copy-done.2
  3.9 0.0 copy-start.3
  3.9 0.8 copy-done.3
  4.7 125.7 %shard_map.68 = (f32[4,16,128]{2,1,0:T(8,128)S(1)}, f32[3,16,128]{2,1,0:T(8,128)S(1)}) custom-call(bf16[1,512,128]{2,1,0:T(8,128)(2,1)S(1)} %bitcast.7, bf16[3,512,128]{2,1,0:T(8,128)(2,1)S(1)} %bitcast.6, f32[4,16,128]{2,1,0:T(8,128)S(1)} %copy-done.2, bf16[16,1024]{1,0:T(8,128)(2,1)S(1)} %bitcast.8, s32[4]{0:T(128)S(1)} %copy-done.4), custom_call_target="tpu_custom_call" | custom-call | tf_op jit(solution)/shard_map/pallas_call | solution.py:304
  130.4 0.6 copy.10
  131.0 0.6 copy.11
Async XLA Ops:
  0.6 0.7 copy-start.4
  1.3 1.0 copy-start
  2.3 0.9 copy-start.1
  3.2 0.8 copy-start.2
  3.9 0.8 copy-start.3

commit v2 on v0

v2 whole, which is shorter than its diff:
```python
import jax
import jax.numpy as jnp
from jax import lax
from jax.experimental import pallas as pl
from jax.experimental.pallas import tpu as pltpu
from jax.sharding import PartitionSpec as P

MESH = pl.DeviceIdType.MESH
FACTOR_DECAY = 0.9
TOKENS = 32768
TOK = 512
PIECES = 4
LANE = 128
ROWS = 16


def gram(lhs8, rhs4, part, j_base):
    rhs = jnp.concatenate([rhs4[j_base + j] for j in range(PIECES)], axis=1)

    def tile(i, _):
        lhs = jnp.concatenate([lhs8[2 * i], lhs8[2 * i + 1]], axis=1)
        out = lax.dot_general(lhs, rhs, (((0,), (0,)), ((), ())), preferred_element_type=jnp.float32)
        for j in range(PIECES):
            part[j, i] = out[:, j * LANE:(j + 1) * LANE].reshape(4, 2, 2, ROWS, LANE)
        return 0

    lax.fori_loop(0, 4, tile, 0)


def kernel(
    act, grads, old, inv, owners, nf_out, pr_out,
    cols, x8, shard, full_inv, s8, a4, old_v,
    part, half, y_out, y_in, mid, near_in, far_out, far_in, fin, frecv,
    loc_sem, xs_sem, xr_sem, is_sem, ir_sem, ns_sem, nr_sem, fs_sem, fr_sem, as_sem, ar_sem, ps_sem, pr_sem,
    ss_sem, sr_sem, bs_sem, br_sem, cs_sem, cr_sem, ys_sem, yr_sem, zs_sem, zr_sem, ws_sem, wr_sem, ts_sem, tr_sem,
):
    dp = lax.axis_index("dp")
    own = lax.axis_index("own")
    z = dp // 4
    k = z // 4
    r = z % 4
    y = (dp // 2) % 2
    c = dp % 2
    h = own // 4
    x = own % 4

    def at(zz, yy, cc):
        return (((zz % 16) * 2 + yy) * 2 + cc, own)

    def member(hh, xx):
        return (dp, hh * 4 + xx)

    core = at(z, y, 1 - c)
    across = at(z, 1 - y, c)
    diagonal = at(z, 1 - y, 1 - c)
    by_z = {d: at(z + d, y, c) for d in (1, 15, 2, 14)}
    far = {d: at(((k + d) % 4) * 4 + r, y, c) for d in (1, 2, 3)}
    peers = [((h + d // 4) % 2, (x + d % 4) % 4) for d in range(8)]

    loc = [
        pltpu.make_async_copy(act, cols.at[pl.ds(0, 1)], loc_sem.at[0]),
        pltpu.make_async_copy(grads, cols.at[pl.ds(1, 3)], loc_sem.at[1]),
        pltpu.make_async_copy(inv.at[:, pl.ds(h * 512, 512)], shard.at[own], loc_sem.at[2]),
        pltpu.make_async_copy(old, old_v, loc_sem.at[3]),
    ]
    for copy in loc:
        copy.start()

    barrier = pltpu.get_barrier_semaphore()
    targets = [member(*peers[d]) for d in range(1, 8)] + [core, across, diagonal]
    targets = targets + list(by_z.values()) + list(far.values())
    for target in targets:
        pl.semaphore_signal(barrier, inc=1, device_id=target, device_id_type=MESH)
    pl.semaphore_wait(barrier, len(targets))

    def remote(src, dst, s_sem, r_sem, target):
        return pltpu.make_async_remote_copy(
            src_ref=src, dst_ref=dst, send_sem=s_sem, recv_sem=r_sem, device_id=target, device_id_type=MESH
        )

    def start(copies):
        for copy in copies:
            copy.start()
        return copies

    inv_copies = start([
        remote(inv.at[:, pl.ds(peers[d][0] * 512, 512)], shard.at[own], is_sem.at[d], ir_sem.at[d], member(*peers[d]))
        for d in (4, 1, 3, 5, 7, 2, 6)
    ])
    loc[0].wait()
    loc[1].wait()
    x_copies = start([
        remote(cols.at[peers[d][1]], x8.at[own], xs_sem.at[d], xr_sem.at[d], member(*peers[d]))
        for d in (4, 1, 6, 3, 5, 2, 7)
    ])
    x8[own] = cols[x]
    loc[2].wait()

    for copy in inv_copies:
        copy.wait_recv()
    full_inv[k, r, y, c] = shard[owners[x]]
    here = full_inv.at[k, r, y, c]
    near_copies = start([
        remote(here, here, ns_sem.at[i], nr_sem.at[i], target) for i, target in enumerate((core, across, diagonal))
    ])
    for copy in near_copies:
        copy.wait_recv()
    here = full_inv.at[k, r, c]
    far_copies = start([remote(here, here, fs_sem.at[d], fr_sem.at[d], far[d]) for d in (2, 1, 3)])

    def pass_copy(i, view):
        return remote(view, view, ps_sem.at[i], pr_sem.at[i], core)

    pass_copies = []
    get_copies = []

    def pass_on(i, view, other):
        pass_copies.append(pass_copy(i, view))
        pass_copies[-1].start()
        get_copies.append(pass_copy(i, other))

    for copy in x_copies:
        copy.wait_recv()
    gram(x8, x8, part.at[0], h * PIECES)

    def core_copy(n, j):
        return remote(part.at[n, j, :, :, :, 1 - c], half.at[n, j], cs_sem.at[n, j], cr_sem.at[n, j], core)

    def y_copy(n, j):
        return remote(y_out.at[n, j], y_in.at[n, j], ys_sem.at[n, j], yr_sem.at[n, j], across)

    def z_copies(n, j):
        two = 2 if j % 2 == 0 else 14
        return [
            remote(mid.at[n, j, :, (r + d) % 4], near_in.at[n, j, i], zs_sem.at[n, j, i], zr_sem.at[n, j, i], by_z[d])
            for i, d in enumerate((two, 1, 15))
        ]

    def w_copies(n, j):
        return [
            remote(far_out.at[n, j, (k + d) % 4], far_in.at[n, j, d - 1], ws_sem.at[n, j, d - 1],
                   wr_sem.at[n, j, d - 1], far[d])
            for d in (2, 1, 3)
        ]

    def final_copy(n, j):
        return remote(fin.at[n, j], frecv.at[n, x], ts_sem.at[n, j], tr_sem.at[n, x], member(h, j))

    def core_start(n):
        for j in range(PIECES):
            core_copy(n, j).start()

    def y_start(n, j):
        core_copy(n, j).wait_recv()
        y_out[n, j] = part[n, j, :, :, 1 - y, c] + half[n, j, :, :, 1 - y]
        y_copy(n, j).start()

    def z_start(n, j):
        y_copy(n, j).wait_recv()
        mid[n, j] = part[n, j, :, :, y, c] + half[n, j, :, :, y] + y_in[n, j]
        start(z_copies(n, j))

    def w_start(n, j):
        for copy in z_copies(n, j):
            copy.wait_recv()
        far_out[n, j] = mid[n, j, :, r] + near_in[n, j, 0] + near_in[n, j, 1] + near_in[n, j, 2]
        start(w_copies(n, j))

    def final_start(n, j):
        for copy in w_copies(n, j):
            copy.wait_recv()
        fin[n, j] = far_out[n, j, k] + far_in[n, j, 0] + far_in[n, j, 1] + far_in[n, j, 2]

        @pl.when(x != j)
        def _():
            final_copy(n, j).start()

        @pl.when(x == j)
        def _():
            frecv[n, j] = fin[n, j]

    def final_wait(n, xx):
        remote(fin.at[n, 0], frecv.at[n, xx], ts_sem.at[n, 0], tr_sem.at[n, xx], member(h, xx)).wait_recv()

    def drain(n):
        for j in range(PIECES):
            core_copy(n, j).wait_send()
            y_copy(n, j).wait_send()
            for copy in z_copies(n, j) + w_copies(n, j):
                copy.wait_send()

            @pl.when(x != j)
            def _():
                final_copy(n, j).wait_send()

    core_start(0)

    for i, (copy, d) in enumerate(zip(far_copies, (2, 1, 3))):
        copy.wait_recv()
    adj_copies = start([
        remote(full_inv.at[pl.ds(0, 2), r, c], full_inv.at[pl.ds(0, 2), r, c], as_sem.at[0], ar_sem.at[0], by_z[2]),
        remote(full_inv.at[pl.ds(2, 2), r, c], full_inv.at[pl.ds(2, 2), r, c], as_sem.at[1], ar_sem.at[1], by_z[14]),
        remote(full_inv.at[:, r, c], full_inv.at[:, r, c], as_sem.at[2], ar_sem.at[2], by_z[1]),
        remote(full_inv.at[:, r, c], full_inv.at[:, r, c], as_sem.at[3], ar_sem.at[3], by_z[15]),
    ])
    for d in (1, 2, 3):
        pass_on(d - 1, full_inv.at[(k + d) % 4, r, c], full_inv.at[(k + d) % 4, r, 1 - c])
    for j in range(PIECES):
        y_start(0, j)
    for i, (ks, d) in enumerate(((pl.ds(0, 4), 3), (pl.ds(0, 4), 1), (pl.ds(0, 2), 2), (pl.ds(2, 2), 2))):
        adj_copies[(2, 3, 0, 1)[i]].wait_recv()
        pass_on(3 + i, full_inv.at[ks, (r + d) % 4, c], full_inv.at[ks, (r + d) % 4, 1 - c])
    for copy in get_copies:
        copy.wait_recv()

    weights = full_inv[...].reshape(1024, 512)

    def scale_tile(i, _):
        rows = pl.ds(pl.multiple_of(i * 256, 256), 256)
        lhs = jnp.concatenate([x8[m, rows, :] for m in range(8)], axis=1)
        out = jnp.dot(lhs, weights, preferred_element_type=jnp.float32).astype(jnp.bfloat16)
        for j in range(PIECES):
            s8[h * PIECES + j, rows, :] = out[:, j * LANE:(j + 1) * LANE]
        return 0

    lax.fori_loop(0, TOK // 256, scale_tile, 0)

    mine = s8.at[pl.ds(h * PIECES, PIECES)]
    swap_copy = remote(mine, mine, ss_sem.at[0], sr_sem.at[0], member(1 - h, x))
    act_copies = [remote(mine, a4, bs_sem.at[g], br_sem.at[0], member(h, g)) for g in range(4)]

    @pl.when(x == 0)
    def _():
        for g in (2, 1, 3):
            act_copies[g].start()

    @pl.when(x > 0)
    def _():
        swap_copy.start()

    for j in range(PIECES):
        z_start(0, j)

    @pl.when(x > 0)
    def _():
        act_copies[0].wait_recv()
        swap_copy.wait_recv()
        gram(s8, a4, part.at[1], 0)
        core_start(1)

    for j in range(PIECES):
        w_start(0, j)

    @pl.when(x > 0)
    def _():
        for j in range(PIECES):
            y_start(1, j)

    for j in range(PIECES):
        final_start(0, j)

    @pl.when(x > 0)
    def _():
        for j in range(PIECES + 1):
            if j < PIECES:
                z_start(1, j)
            if j > 0:
                w_start(1, j - 1)
        for j in range(PIECES):
            final_start(1, j)

    loc[3].wait()
    for d in (1, 2, 3):
        final_wait(0, (x + d) % 4)
    nf_out[...] = FACTOR_DECAY * old_v[...] + ((1.0 - FACTOR_DECAY) / TOKENS) * frecv[0]

    for d in (1, 2, 3):
        @pl.when((x + d) % 4 > 0)
        def _():
            final_wait(1, (x + d) % 4)
    pr_out[...] = frecv[1, 1:4] * (1.0 / TOKENS)

    for copy in inv_copies + x_copies + near_copies + far_copies + adj_copies + pass_copies:
        copy.wait_send()
    drain(0)

    @pl.when(x == 0)
    def _():
        for g in (1, 2, 3):
            act_copies[g].wait_send()

    @pl.when(x > 0)
    def _():
        swap_copy.wait_send()
        drain(1)


def body(activations, output_grads, old_factors, inverses, owners):
    vmem = pl.BlockSpec(memory_space=pltpu.VMEM)
    hbm = pl.BlockSpec(memory_space=pl.ANY)
    bf16, f32 = jnp.bfloat16, jnp.float32
    dma = lambda *shape: pltpu.SemaphoreType.DMA(shape)
    new_factors, preconditioned = pl.pallas_call(
        kernel,
        out_shape=(
            jax.ShapeDtypeStruct((4, ROWS, LANE), f32),
            jax.ShapeDtypeStruct((3, ROWS, LANE), f32),
        ),
        in_specs=[hbm, hbm, hbm, hbm, pl.BlockSpec(memory_space=pltpu.SMEM)],
        out_specs=(vmem, vmem),
        scratch_shapes=[
            pltpu.VMEM((4, TOK, LANE), bf16),
            pltpu.VMEM((8, TOK, LANE), bf16),
            pltpu.VMEM((8, ROWS, 512), bf16),
            pltpu.VMEM((4, 4, 2, 2, ROWS, 512), bf16),
            pltpu.VMEM((8, TOK, LANE), bf16),
            pltpu.VMEM((4, TOK, LANE), bf16),
            pltpu.VMEM((4, ROWS, LANE), f32),
            pltpu.VMEM((2, PIECES, 4, 4, 2, 2, ROWS, LANE), f32),
            pltpu.VMEM((2, PIECES, 4, 4, 2, ROWS, LANE), f32),
            pltpu.VMEM((2, PIECES, 4, 4, ROWS, LANE), f32),
            pltpu.VMEM((2, PIECES, 4, 4, ROWS, LANE), f32),
            pltpu.VMEM((2, PIECES, 4, 4, ROWS, LANE), f32),
            pltpu.VMEM((2, PIECES, 3, 4, ROWS, LANE), f32),
            pltpu.VMEM((2, PIECES, 4, ROWS, LANE), f32),
            pltpu.VMEM((2, PIECES, 3, ROWS, LANE), f32),
            pltpu.VMEM((2, PIECES, ROWS, LANE), f32),
            pltpu.VMEM((2, PIECES, ROWS, LANE), f32),
            dma(4),
            dma(8), dma(8), dma(8), dma(8), dma(3), dma(3), dma(4), dma(4), dma(4), dma(4), dma(7), dma(7),
            dma(1), dma(1), dma(4), dma(1), dma(2, 4), dma(2, 4), dma(2, 4), dma(2, 4),
            dma(2, 4, 3), dma(2, 4, 3), dma(2, 4, 3), dma(2, 4, 3), dma(2, 4), dma(2, 4),
        ],
        compiler_params=pltpu.CompilerParams(
            collective_id=0, has_side_effects=True, vmem_limit_bytes=56 * 1024 * 1024
        ),
    )(
        jnp.swapaxes(activations, 0, 1),
        jnp.swapaxes(output_grads, 0, 1),
        old_factors,
        inverses.reshape(ROWS, 1024),
        owners,
    )
    return new_factors, preconditioned.reshape(3, ROWS, 1, LANE)


def solution(mesh):
    placed = (
        P("dp", None, "own"),
        P("dp", None, "own"),
        P(None, "dp", "own"),
        P("own", None, "dp", None),
        P(),
    )
    return jax.shard_map(
        body,
        mesh=mesh,
        in_specs=placed,
        out_specs=(P(None, "dp", "own"), P(None, "dp", None, "own")),
        check_vma=False,
    )
```

time: 845 us -> 113 us (0.13)
  waiting for transfers between devices: 781 us -> 0 us
  Pallas kernels: 0 us -> 110 us
  matrix products: 20.6 us -> 0 us
  between operations: 13.9 us -> 0.65 us
  other arithmetic: 10.7 us -> 0 us
    reduce_scatter x2 -> x0, waiting for transfers between devices: 450 us -> none  [the longest x1 226 us: body(): lax.psum_scatter(gradient_term, 'dp', scatter_dimension=1, tiled=True)]
    all_gather x3 -> x0, waiting for transfers between devices: 316 us -> none  [the longest x1 118 us: body(): rows_full = lax.all_gather(inverses, 'dp', axis=2, tiled=True)[0]]
    pallas_call x0 -> x1, Pallas kernels: none -> 110 us  [body(): pl.pallas_call(kernel, out_shape=(jax.ShapeDtypeStruct((4, ROWS, LANE), f...]
    dot_general x5 -> x0, matrix products: 20.6 us -> none  [the longest x1 6.62 us: body(): jnp.einsum('uoi,uns->oins', lax.all_gather(grad_cols, 'own', axis=2, tile...]
    all_to_all x1 -> x0, waiting for transfers between devices: 14.9 us -> none  [body(): lax.all_to_all(product, 'own', split_axis=2, concat_axis=0, tiled=True)]
  transfers between devices with their start and end apart: 6 -> 0, of which waited for: 6 -> 0; matrix products, arithmetic and copies ran while one was open for 2% -> 0% of each run, Pallas kernels for 0% -> 0%
where the time goes in v2:
time: 113 us
  Pallas kernels  110 us (97%)
  local copies, waits for them, and re-layouts  1.99 us (2%)
    pallas_call x1, Pallas kernels, body(): pl.pallas_call(kernel, out_shape=(jax.ShapeDtypeStruct((4, ROWS, LANE), f...  110 us

profile of v2, /device:TPU:6, one launch (start us, length us, event | category | flops | bytes accessed | tf_op | source)
XLA Modules:
  0.0 113.0 jit_solution(4850647332666796144)
XLA Ops:
  0.6 110.3 %shard_map.68 = (f32[4,16,128]{2,1,0:T(8,128)}, f32[3,16,128]{2,1,0:T(8,128)}) custom-call(bf16[1,512,128]{2,1,0:T(8,128)(2,1)} %bitcast.7, bf16[3,512,128]{2,1,0:T(8,128)(2,1)} %bitcast.6, f32[4,16,128]{2,1,0:T(8,128)} %old.1, bf16[16,1024]{1,0:T(8,128)(2,1)} %bitcast.8, s32[4]{0:T(128)} %owners.1), custom_call_target="tpu_custom_call" | custom-call | tf_op jit(solution)/shard_map/pallas_call | solution.py:303
  111.0 0.0 copy-start
  111.0 1.4 %copy.10 = f32[4,16,128]{2,1,0:T(8,128)} copy(f32[4,16,128]{2,1,0:T(8,128)} %get-tuple-element.10) | data formatting | bytes 65536
  112.4 0.0 copy-done
  112.4 0.6 copy.11
Async XLA Ops:
  111.0 1.4 %copy-start = (f32[3,16,128]{2,1,0:T(8,128)S(1)}, f32[3,16,128]{2,1,0:T(8,128)}, u32[]{:S(2)}) copy-start(f32[3,16,128]{2,1,0:T(8,128)} %get-tuple-element.5) | copy-start | bytes 73732

commit v3 on v2

v3 whole, which is shorter than its diff:
```python
import jax
import jax.numpy as jnp
from jax import lax
from jax.experimental import pallas as pl
from jax.experimental.pallas import tpu as pltpu
from jax.sharding import PartitionSpec as P

MESH = pl.DeviceIdType.MESH
FACTOR_DECAY = 0.9
TOKENS = 32768
TOK = 512
PIECES = 4
LANE = 128
ROWS = 16


def gram(lhs8, rhs4, part, j_base):
    rhs = jnp.concatenate([rhs4[j_base + j] for j in range(PIECES)], axis=1)

    def tile(i, _):
        lhs = jnp.concatenate([lhs8[2 * i], lhs8[2 * i + 1]], axis=1)
        out = lax.dot_general(lhs, rhs, (((0,), (0,)), ((), ())), preferred_element_type=jnp.float32)
        for j in range(PIECES):
            part[j, i] = out[:, j * LANE:(j + 1) * LANE].reshape(4, 2, 2, ROWS, LANE)
        return 0

    lax.fori_loop(0, 4, tile, 0)


def kernel(
    act, grads, old, inv, owners, nf_out, pr_out,
    cols, x8, shard, full_inv, s8, a4, old_v, part, half,
    mid_c, near_c, out_c, in_c, sum_c, cross_c,
    y_out, y_in, mid_p, near_p, out_p, in_p,
    loc_sem, xs_sem, xr_sem, is_sem, ir_sem, ns_sem, nr_sem, fs_sem, fr_sem, as_sem, ar_sem, ps_sem, pr_sem,
    ss_sem, sr_sem, bs_sem, br_sem, cs_sem, cr_sem, ys_sem, yr_sem, zs_sem, zr_sem, ws_sem, wr_sem, ts_sem, tr_sem,
):
    dp = lax.axis_index("dp")
    own = lax.axis_index("own")
    z = dp // 4
    k = z // 4
    r = z % 4
    y = (dp // 2) % 2
    c = dp % 2
    h = own // 4
    x = own % 4

    def at(zz, yy, cc, mm):
        return (((zz % 16) * 2 + yy) * 2 + cc, mm)

    def member(hh, xx):
        return (dp, hh * 4 + xx)

    def far(d, xx):
        return at(((k + d) % 4) * 4 + r, y, c, h * 4 + xx)

    core = at(z, y, 1 - c, own)
    across = at(z, 1 - y, c, own)
    diagonal = at(z, 1 - y, 1 - c, own)
    by_z = {d: at(z + d, y, c, own) for d in (1, 15, 2, 14)}
    peers = [((h + d // 4) % 2, (x + d % 4) % 4) for d in range(8)]

    loc = [
        pltpu.make_async_copy(act, cols.at[pl.ds(0, 1)], loc_sem.at[0]),
        pltpu.make_async_copy(grads, cols.at[pl.ds(1, 3)], loc_sem.at[1]),
        pltpu.make_async_copy(inv.at[:, pl.ds(h * 512, 512)], shard.at[own], loc_sem.at[2]),
        pltpu.make_async_copy(old, old_v, loc_sem.at[3]),
    ]
    for copy in loc:
        copy.start()

    barrier = pltpu.get_barrier_semaphore()
    targets = [far(d, (x + e) % 4) for d in (2, 1, 3) for e in range(4)] + list(by_z.values())
    targets = targets + [member(*peers[d]) for d in range(1, 8)] + [core, across, diagonal]
    for target in targets:
        pl.semaphore_signal(barrier, inc=1, device_id=target, device_id_type=MESH)
    pl.semaphore_wait(barrier, len(targets))

    def remote(src, dst, s_sem, r_sem, target):
        return pltpu.make_async_remote_copy(
            src_ref=src, dst_ref=dst, send_sem=s_sem, recv_sem=r_sem, device_id=target, device_id_type=MESH
        )

    def start(copies):
        for copy in copies:
            copy.start()
        return copies

    inv_copies = start([
        remote(inv.at[:, pl.ds(peers[d][0] * 512, 512)], shard.at[own], is_sem.at[d], ir_sem.at[d], member(*peers[d]))
        for d in (4, 1, 3, 5, 7, 2, 6)
    ])
    loc[2].wait()
    for copy in inv_copies:
        copy.wait_recv()

    mine = shard[owners[x]]
    for u in range(2):
        full_inv[u, k, r, y, c] = mine[:, u * 256:(u + 1) * 256]
    here = full_inv.at[:, k, r, y, c]
    near_copies = start([
        remote(here, here, ns_sem.at[i], nr_sem.at[i], target) for i, target in enumerate((across, diagonal, core))
    ])

    loc[0].wait()
    loc[1].wait()
    x_copies = start([
        remote(cols.at[peers[d][1]], x8.at[own], xs_sem.at[d], xr_sem.at[d], member(*peers[d]))
        for d in (4, 1, 6, 3, 5, 2, 7)
    ])
    x8[own] = cols[x]

    for copy in near_copies:
        copy.wait_recv()

    def far_copy(u, d):
        view = full_inv.at[u, k, r, c]
        return remote(view, view, fs_sem.at[u, d], fr_sem.at[u, d], far(d, x))

    def adj_copy(u, i):
        view = (full_inv.at[u, pl.ds(0, 2), r, c], full_inv.at[u, pl.ds(2, 2), r, c], full_inv.at[u, :, r, c],
                full_inv.at[u, :, r, c])[i]
        return remote(view, view, as_sem.at[u, i], ar_sem.at[u, i], by_z[(2, 14, 1, 15)[i]])

    def pass_views(u, cc):
        views = [full_inv.at[u, (k + d) % 4, r, cc] for d in (1, 2, 3)]
        return views + [
            full_inv.at[u, pl.ds(0, 2), (r + 2) % 4, cc], full_inv.at[u, pl.ds(2, 2), (r + 2) % 4, cc],
            full_inv.at[u, :, (r + 3) % 4, cc], full_inv.at[u, :, (r + 1) % 4, cc],
        ]

    def pass_copy(u, i, cc):
        view = pass_views(u, cc)[i]
        return remote(view, view, ps_sem.at[u, i], pr_sem.at[u, i], core)

    for u in range(2):
        for d in (2, 1, 3):
            far_copy(u, d).start()
    for u in range(2):
        for d in (2, 1, 3):
            far_copy(u, d).wait_recv()
        for i in range(4):
            adj_copy(u, i).start()
        for i in range(3):
            pass_copy(u, i, c).start()

    for copy in x_copies:
        copy.wait_recv()
    gram(x8, x8, part.at[0], h * PIECES)

    def core_copy(n, j):
        return remote(part.at[n, j, :, :, :, 1 - c], half.at[n, j], cs_sem.at[n, j], cr_sem.at[n, j], core)

    for j in range(PIECES):
        core_copy(0, j).start()

    def scale(u):
        for i in range(4):
            adj_copy(u, i).wait_recv()
            pass_copy(u, 3 + i, c).start()
        for i in range(7):
            pass_copy(u, i, 1 - c).wait_recv()
        weights = full_inv[u].reshape(1024, 256)

        def tile(i, _):
            rows = pl.ds(pl.multiple_of(i * 256, 256), 256)
            lhs = jnp.concatenate([x8[m, rows, :] for m in range(8)], axis=1)
            out = jnp.dot(lhs, weights, preferred_element_type=jnp.float32).astype(jnp.bfloat16)
            for j in range(2):
                s8[h * PIECES + 2 * u + j, rows, :] = out[:, j * LANE:(j + 1) * LANE]
            return 0

        lax.fori_loop(0, TOK // 256, tile, 0)

    def swap_copy(u):
        view = s8.at[pl.ds(h * PIECES + 2 * u, 2)]
        return remote(view, view, ss_sem.at[u], sr_sem.at[u], member(1 - h, x))

    def act_copy(j, g):
        return remote(s8.at[h * PIECES + j], a4.at[j], bs_sem.at[j, g // 2], br_sem.at[j], member(h, g))

    def hand_copy(j):
        return remote(a4.at[j], a4.at[j], bs_sem.at[j, 0], br_sem.at[j], member(h, 2))

    def scaled_start(u):
        @pl.when(x == 0)
        def _():
            for i in range(2):
                act_copy(2 * u + i, 1).start()
                act_copy(2 * u + 1 - i, 3).start()

        @pl.when(x > 0)
        def _():
            swap_copy(u).start()

    def hand_on(u):
        for i, g in enumerate((1, 3)):
            @pl.when(x == g)
            def _():
                hand_copy(2 * u + i).wait_recv()
                hand_copy(2 * u + i).start()

    def two_away(j):
        return 2 if j % 2 == 0 else 14

    def near_c_copies(j):
        return [
            remote(mid_c.at[j, :, (r + d) % 4], near_c.at[j, i], zs_sem.at[0, j, i], zr_sem.at[0, j, i], by_z[d])
            for i, d in enumerate((two_away(j), 1, 15))
        ]

    def near_c_start(j):
        core_copy(0, j).wait_recv()
        mid_c[j] = part[0, j, :, :, :, c] + half[0, j]
        start(near_c_copies(j))

    def out_copy(n, out, dst, j, d):
        return remote(out.at[j, (k + d) % 4], dst.at[x, d], ws_sem.at[n, j, d], wr_sem.at[n, x, d], far(d, j))

    def out_start(n, out, dst, j):
        for d in (2, 1, 3):
            out_copy(n, out, dst, j, d).start()

        @pl.when(x != j)
        def _():
            out_copy(n, out, dst, j, 0).start()

        @pl.when(x == j)
        def _():
            dst[j, 0] = out[j, k]

    def out_wait(n, out, dst, xx):
        def arrived(d):
            remote(out.at[0, 0], dst.at[xx, d], ws_sem.at[n, 0, d], wr_sem.at[n, xx, d], far(d, xx)).wait_recv()

        for d in (1, 2, 3):
            arrived(d)

        @pl.when(x != xx)
        def _():
            arrived(0)

    def out_drain(n, out, dst):
        for j in range(PIECES):
            for d in (1, 2, 3):
                out_copy(n, out, dst, j, d).wait_send()

            @pl.when(x != j)
            def _():
                out_copy(n, out, dst, j, 0).wait_send()

    def out_c_start(j):
        for copy in near_c_copies(j):
            copy.wait_recv()
        out_c[j] = mid_c[j, :, r] + near_c[j, 0] + near_c[j, 1] + near_c[j, 2]
        out_start(0, out_c, in_c, j)

    cross_copy = remote(sum_c.at[:, 1 - y], cross_c, ts_sem.at[0], tr_sem.at[0], across)

    def y_copy(j):
        return remote(y_out.at[j], y_in.at[j], ys_sem.at[j], yr_sem.at[j], across)

    def near_p_copies(j):
        return [
            remote(mid_p.at[j, :, (r + d) % 4], near_p.at[j, i], zs_sem.at[1, j, i], zr_sem.at[1, j, i], by_z[d])
            for i, d in enumerate((two_away(j), 1, 15))
        ]

    def y_start(j):
        core_copy(1, j).wait_recv()
        y_out[j] = part[1, j, :, :, 1 - y, c] + half[1, j, :, :, 1 - y]
        y_copy(j).start()

    def near_p_start(j):
        y_copy(j).wait_recv()
        mid_p[j] = part[1, j, :, :, y, c] + half[1, j, :, :, y] + y_in[j]
        start(near_p_copies(j))

    def out_p_start(j):
        for copy in near_p_copies(j):
            copy.wait_recv()
        out_p[j] = mid_p[j, :, r] + near_p[j, 0] + near_p[j, 1] + near_p[j, 2]
        out_start(1, out_p, in_p, j)

    scale(0)
    scaled_start(0)
    scale(1)
    scaled_start(1)
    for j in range(PIECES):
        near_c_start(j)
    hand_on(0)
    hand_on(1)
    for j in range(2):
        out_c_start(j)

    @pl.when(x > 0)
    def _():
        for u in range(2):
            swap_copy(u).wait_recv()
            for i, g in enumerate((1, 3)):
                @pl.when(x != g)
                def _():
                    act_copy(2 * u + i, 1).wait_recv()
        gram(s8, a4, part.at[1], 0)
        for j in range(PIECES):
            core_copy(1, j).start()
        for j in range(PIECES):
            y_start(j)

    for j in range(2, PIECES):
        out_c_start(j)

    @pl.when(x > 0)
    def _():
        near_p_start(0)

    for xx in range(PIECES):
        out_wait(0, out_c, in_c, xx)
        sum_c[xx] = in_c[xx, 0] + in_c[xx, 1] + in_c[xx, 2] + in_c[xx, 3]
    cross_copy.start()

    @pl.when(x > 0)
    def _():
        for j in range(1, PIECES + 1):
            if j < PIECES:
                near_p_start(j)
            out_p_start(j - 1)

    cross_copy.wait_recv()
    loc[3].wait()
    total = sum_c[:, y] + cross_c[...]
    nf_out[...] = FACTOR_DECAY * old_v[...] + ((1.0 - FACTOR_DECAY) / TOKENS) * total

    for xx in range(1, PIECES):
        out_wait(1, out_p, in_p, xx)
        pr_out[xx - 1] = (in_p[xx, 0] + in_p[xx, 1] + in_p[xx, 2] + in_p[xx, 3]) * (1.0 / TOKENS)

    for copy in inv_copies + x_copies + near_copies + [cross_copy]:
        copy.wait_send()
    for u in range(2):
        for d in (1, 2, 3):
            far_copy(u, d).wait_send()
        for i in range(4):
            adj_copy(u, i).wait_send()
        for i in range(7):
            pass_copy(u, i, c).wait_send()
    for j in range(PIECES):
        core_copy(0, j).wait_send()
        for copy in near_c_copies(j):
            copy.wait_send()
    out_drain(0, out_c, in_c)

    @pl.when(x == 0)
    def _():
        for j in range(PIECES):
            act_copy(j, 1).wait_send()
            act_copy(j, 3).wait_send()

    for i, g in enumerate((1, 3)):
        @pl.when(x == g)
        def _():
            for u in range(2):
                hand_copy(2 * u + i).wait_send()

    @pl.when(x > 0)
    def _():
        for u in range(2):
            swap_copy(u).wait_send()
        for j in range(PIECES):
            core_copy(1, j).wait_send()
            y_copy(j).wait_send()
            for copy in near_p_copies(j):
                copy.wait_send()
        out_drain(1, out_p, in_p)


def body(activations, output_grads, old_factors, inverses, owners):
    vmem = pl.BlockSpec(memory_space=pltpu.VMEM)
    hbm = pl.BlockSpec(memory_space=pl.ANY)
    bf16, f32 = jnp.bfloat16, jnp.float32
    dma = lambda *shape: pltpu.SemaphoreType.DMA(shape)
    new_factors, preconditioned = pl.pallas_call(
        kernel,
        out_shape=(
            jax.ShapeDtypeStruct((4, ROWS, LANE), f32),
            jax.ShapeDtypeStruct((3, ROWS, LANE), f32),
        ),
        in_specs=[hbm, hbm, hbm, hbm, pl.BlockSpec(memory_space=pltpu.SMEM)],
        out_specs=(vmem, vmem),
        scratch_shapes=[
            pltpu.VMEM((4, TOK, LANE), bf16),
            pltpu.VMEM((8, TOK, LANE), bf16),
            pltpu.VMEM((8, ROWS, 512), bf16),
            pltpu.VMEM((2, 4, 4, 2, 2, ROWS, 256), bf16),
            pltpu.VMEM((8, TOK, LANE), bf16),
            pltpu.VMEM((4, TOK, LANE), bf16),
            pltpu.VMEM((4, ROWS, LANE), f32),
            pltpu.VMEM((2, PIECES, 4, 4, 2, 2, ROWS, LANE), f32),
            pltpu.VMEM((2, PIECES, 4, 4, 2, ROWS, LANE), f32),
            pltpu.VMEM((PIECES, 4, 4, 2, ROWS, LANE), f32),
            pltpu.VMEM((PIECES, 3, 4, 2, ROWS, LANE), f32),
            pltpu.VMEM((PIECES, 4, 2, ROWS, LANE), f32),
            pltpu.VMEM((PIECES, 4, 2, ROWS, LANE), f32),
            pltpu.VMEM((PIECES, 2, ROWS, LANE), f32),
            pltpu.VMEM((PIECES, ROWS, LANE), f32),
            pltpu.VMEM((PIECES, 4, 4, ROWS, LANE), f32),
            pltpu.VMEM((PIECES, 4, 4, ROWS, LANE), f32),
            pltpu.VMEM((PIECES, 4, 4, ROWS, LANE), f32),
            pltpu.VMEM((PIECES, 3, 4, ROWS, LANE), f32),
            pltpu.VMEM((PIECES, 4, ROWS, LANE), f32),
            pltpu.VMEM((PIECES, 4, ROWS, LANE), f32),
            dma(4),
            dma(8), dma(8), dma(8), dma(8), dma(3), dma(3), dma(2, 4), dma(2, 4), dma(2, 4), dma(2, 4), dma(2, 7),
            dma(2, 7), dma(2), dma(2), dma(4, 2), dma(4), dma(2, 4), dma(2, 4), dma(4), dma(4),
            dma(2, 4, 3), dma(2, 4, 3), dma(2, 4, 4), dma(2, 4, 4), dma(1), dma(1),
        ],
        compiler_params=pltpu.CompilerParams(
            collective_id=0, has_side_effects=True, vmem_limit_bytes=56 * 1024 * 1024
        ),
    )(
        jnp.swapaxes(activations, 0, 1),
        jnp.swapaxes(output_grads, 0, 1),
        old_factors,
        inverses.reshape(ROWS, 1024),
        owners,
    )
    return new_factors, preconditioned.reshape(3, ROWS, 1, LANE)


def solution(mesh):
    placed = (
        P("dp", None, "own"),
        P("dp", None, "own"),
        P(None, "dp", "own"),
        P("own", None, "dp", None),
        P(),
    )
    return jax.shard_map(
        body,
        mesh=mesh,
        in_specs=placed,
        out_specs=(P(None, "dp", "own"), P(None, "dp", None, "own")),
        check_vma=False,
    )
```

time: 113 us -> 97 us (0.86)
  Pallas kernels: 110 us -> 94.2 us
    pallas_call x1, Pallas kernels: 110 us -> 94.2 us  [body(): pl.pallas_call(kernel, out_shape=(jax.ShapeDtypeStruct((4, ROWS, LANE), f...]
where the time goes in v3:
time: 97 us; the launch traced here: 96.8 us
  Pallas kernels  94.2 us (97%)
  local copies, waits for them, and re-layouts  1.99 us (2%)
    pallas_call x1, Pallas kernels, body(): pl.pallas_call(kernel, out_shape=(jax.ShapeDtypeStruct((4, ROWS, LANE), f...  94.2 us
    unnamed x4, local copies, waits for them, and re-layouts  1.99 us

profile of v3, /device:TPU:6, one launch (start us, length us, event | category | flops | bytes accessed | tf_op | source)
XLA Modules:
  0.0 96.8 jit_solution(18207352121070591536)
XLA Ops:
  0.6 94.2 %shard_map.68 = (f32[4,16,128]{2,1,0:T(8,128)}, f32[3,16,128]{2,1,0:T(8,128)}) custom-call(bf16[1,512,128]{2,1,0:T(8,128)(2,1)} %bitcast.7, bf16[3,512,128]{2,1,0:T(8,128)(2,1)} %bitcast.6, f32[4,16,128]{2,1,0:T(8,128)} %old.1, bf16[16,1024]{1,0:T(8,128)(2,1)} %bitcast.8, s32[4]{0:T(128)} %owners.1), custom_call_target="tpu_custom_call" | custom-call | tf_op jit(solution)/shard_map/pallas_call | solution.py:382
  94.8 0.0 copy-start
  94.8 1.4 %copy.10 = f32[4,16,128]{2,1,0:T(8,128)} copy(f32[4,16,128]{2,1,0:T(8,128)} %get-tuple-element.10) | data formatting | bytes 65536
  96.2 0.0 copy-done
  96.2 0.6 copy.11
Async XLA Ops:
  94.8 1.4 %copy-start = (f32[3,16,128]{2,1,0:T(8,128)S(1)}, f32[3,16,128]{2,1,0:T(8,128)}, u32[]{:S(2)}) copy-start(f32[3,16,128]{2,1,0:T(8,128)} %get-tuple-element.5) | copy-start | bytes 73732

commit v4 on v3

v4 whole, which is shorter than its diff:
```python
import jax
import jax.numpy as jnp
from jax import lax
from jax.experimental import pallas as pl
from jax.experimental.pallas import tpu as pltpu
from jax.sharding import PartitionSpec as P

MESH = pl.DeviceIdType.MESH
FACTOR_DECAY = 0.9
TOKENS = 32768
TOK = 512
PIECES = 4
LANE = 128
ROWS = 16


def gram(lhs8, rhs4, part, j_base):
    rhs = jnp.concatenate([rhs4[j_base + j] for j in range(PIECES)], axis=1)

    def tile(i, _):
        lhs = jnp.concatenate([lhs8[2 * i], lhs8[2 * i + 1]], axis=1)
        out = lax.dot_general(lhs, rhs, (((0,), (0,)), ((), ())), preferred_element_type=jnp.float32)
        for j in range(PIECES):
            part[j, i] = out[:, j * LANE:(j + 1) * LANE].reshape(4, 2, 2, ROWS, LANE)
        return 0

    lax.fori_loop(0, 4, tile, 0)


def kernel(
    act, grads, old, inv, owners, nf_out, pr_out,
    cols, x8, shard, full_inv, s8, a4, old_v, part, half,
    mid_z, near_z, out_z, in_z, sum_z, cross_in,
    y_out, y_in, mid_y, near_y, out_y, in_y,
    loc_sem, xs_sem, xr_sem, is_sem, ir_sem, ns_sem, nr_sem, fs_sem, fr_sem, as_sem, ar_sem, ps_sem, pr_sem,
    ss_sem, sr_sem, bs_sem, br_sem, cs_sem, cr_sem, ys_sem, yr_sem, zs_sem, zr_sem, ws_sem, wr_sem, ts_sem, tr_sem,
    chain_2, chain_4,
):
    dp = lax.axis_index("dp")
    own = lax.axis_index("own")
    z = dp // 4
    k = z // 4
    r = z % 4
    y = (dp // 2) % 2
    c = dp % 2
    h = own // 4
    x = own % 4

    def at(zz, yy, cc, mm):
        return (((zz % 16) * 2 + yy) * 2 + cc, mm)

    def member(hh, xx):
        return (dp, hh * 4 + xx)

    def far(d, xx):
        return at(((k + d) % 4) * 4 + r, y, c, h * 4 + xx)

    core = at(z, y, 1 - c, own)
    across = at(z, 1 - y, c, own)
    diagonal = at(z, 1 - y, 1 - c, own)
    by_z = {d: at(z + d, y, c, own) for d in (1, 15, 2, 14)}
    peers = [((h + d // 4) % 2, (x + d % 4) % 4) for d in range(8)]

    loc = [
        pltpu.make_async_copy(act, cols.at[pl.ds(0, 1)], loc_sem.at[0]),
        pltpu.make_async_copy(grads, cols.at[pl.ds(1, 3)], loc_sem.at[1]),
        pltpu.make_async_copy(inv.at[:, pl.ds(h * 512, 512)], shard.at[own], loc_sem.at[2]),
        pltpu.make_async_copy(old, old_v, loc_sem.at[3]),
    ]
    for copy in loc:
        copy.start()

    barrier = pltpu.get_barrier_semaphore()
    targets = list(by_z.values()) + [member(*peers[d]) for d in range(1, 8)] + [core, across, diagonal]
    for target in targets:
        pl.semaphore_signal(barrier, inc=1, device_id=target, device_id_type=MESH)
    pl.semaphore_wait(barrier, len(targets))
    for d in (2, 14):
        pl.semaphore_signal(chain_2, inc=1, device_id=by_z[d], device_id_type=MESH)

    def remote(src, dst, s_sem, r_sem, target):
        return pltpu.make_async_remote_copy(
            src_ref=src, dst_ref=dst, send_sem=s_sem, recv_sem=r_sem, device_id=target, device_id_type=MESH
        )

    def start(copies):
        for copy in copies:
            copy.start()
        return copies

    inv_copies = start([
        remote(inv.at[:, pl.ds(peers[d][0] * 512, 512)], shard.at[own], is_sem.at[d], ir_sem.at[d], member(*peers[d]))
        for d in (4, 1, 3, 5, 7, 2, 6)
    ])
    pl.semaphore_wait(chain_2, 2)
    for d in (1, 3):
        pl.semaphore_signal(chain_4, inc=1, device_id=far(d, x), device_id_type=MESH)
    loc[2].wait()
    for copy in inv_copies:
        copy.wait_recv()

    mine = shard[owners[x]]
    for u in range(2):
        full_inv[u, k, r, y, c] = mine[:, u * 256:(u + 1) * 256]
    here = full_inv.at[:, k, r, y, c]
    near_copies = start([
        remote(here, here, ns_sem.at[i], nr_sem.at[i], target) for i, target in enumerate((across, diagonal, core))
    ])

    loc[0].wait()
    loc[1].wait()
    x_copies = start([
        remote(cols.at[peers[d][1]], x8.at[own], xs_sem.at[d], xr_sem.at[d], member(*peers[d]))
        for d in (4, 1, 6, 3, 5, 2, 7)
    ])
    x8[own] = cols[x]

    for copy in near_copies:
        copy.wait_recv()

    def far_copy(u, d):
        view = full_inv.at[u, k, r, c]
        return remote(view, view, fs_sem.at[u, d], fr_sem.at[u, d], far(d, x))

    def adj_copy(u, d, i):
        b = (k + d) % 4
        view = full_inv.at[u, b, r, c]
        if i < 2:
            target = by_z[(1, 15)[i]]
        else:
            target = at(z + 2 + (b // 2) * 12, y, c, own)
        return remote(view, view, as_sem.at[u, d, i], ar_sem.at[u, b, i], target)

    def adj_wait(u, i):
        for b in range(4):
            view = full_inv.at[u, b, (r + (3, 1, 2)[i]) % 4, c]
            remote(view, view, as_sem.at[u, 0, i], ar_sem.at[u, b, i], by_z[1]).wait_recv()

    def pass_views(u, cc):
        views = [full_inv.at[u, (k + d) % 4, r, cc] for d in (1, 2, 3)]
        return views + [
            full_inv.at[u, :, (r + 3) % 4, cc], full_inv.at[u, :, (r + 1) % 4, cc], full_inv.at[u, :, (r + 2) % 4, cc],
        ]

    def pass_copy(u, i, cc):
        view = pass_views(u, cc)[i]
        return remote(view, view, ps_sem.at[u, i], pr_sem.at[u, i], core)

    pl.semaphore_wait(chain_4, 2)
    for u in range(2):
        for d in (2, 1, 3):
            far_copy(u, d).start()
    for u in range(2):
        for i in range(3):
            adj_copy(u, 0, i).start()
    for d in (1, 3, 2):
        for u in range(2):
            far_copy(u, d).wait_recv()
            for i in range(3):
                adj_copy(u, 4 - d, i).start()
            pass_copy(u, 3 - d, c).start()

    for copy in x_copies:
        copy.wait_recv()
    gram(x8, x8, part.at[0], h * PIECES)

    def piece(i):
        return (x + i) % 4

    def core_copy(n, i):
        j = piece(i)
        return remote(part.at[n, j, :, :, :, 1 - c], half.at[n, j], cs_sem.at[n, i], cr_sem.at[n, i], core)

    for i in (3, 0, 1, 2):
        core_copy(0, i).start()

    def z_first(n, i):
        return n == 0 and i < 3

    def slot(n, i):
        return i if z_first(n, i) else i + 1 if n == 1 else 0

    def y_copy(n, i):
        q = slot(n, i)
        return remote(y_out.at[q], y_in.at[q], ys_sem.at[q], yr_sem.at[q], across)

    def y_start(n, i):
        j = piece(i)
        core_copy(n, i).wait_recv()
        y_out[slot(n, i)] = part[n, j, :, :, 1 - y, c] + half[n, j, :, :, 1 - y]
        if n == 1 and i > 0:
            y_copy(n, i - 1).wait_send()
        y_copy(n, i).start()

    y_start(0, 3)

    def scale(u):
        for i in range(3):
            adj_wait(u, i)
            pass_copy(u, 3 + i, c).start()
        for i in range(6):
            pass_copy(u, i, 1 - c).wait_recv()
        weights = full_inv[u].reshape(1024, 256)

        def tile(i, _):
            rows = pl.ds(pl.multiple_of(i * 256, 256), 256)
            lhs = jnp.concatenate([x8[m, rows, :] for m in range(8)], axis=1)
            out = jnp.dot(lhs, weights, preferred_element_type=jnp.float32).astype(jnp.bfloat16)
            for j in range(2):
                s8[h * PIECES + 2 * u + j, rows, :] = out[:, j * LANE:(j + 1) * LANE]
            return 0

        lax.fori_loop(0, TOK // 256, tile, 0)

    def swap_copy(u):
        view = s8.at[pl.ds(h * PIECES + 2 * u, 2)]
        return remote(view, view, ss_sem.at[u], sr_sem.at[u], member(1 - h, x))

    def act_copy(j, g):
        return remote(s8.at[h * PIECES + j], a4.at[j], bs_sem.at[j, g // 2], br_sem.at[j], member(h, g))

    def hand_copy(j):
        return remote(a4.at[j], a4.at[j], bs_sem.at[j, 0], br_sem.at[j], member(h, 2))

    def scaled_start(u):
        @pl.when(x == 0)
        def _():
            for i in range(2):
                act_copy(2 * u + i, 1).start()
                act_copy(2 * u + 1 - i, 3).start()

        @pl.when(x > 0)
        def _():
            swap_copy(u).start()

    def hand_on(u):
        for i, g in enumerate((1, 3)):
            @pl.when(x == g)
            def _():
                hand_copy(2 * u + i).wait_recv()
                hand_copy(2 * u + i).start()

    def buffers(n, i):
        return (mid_z, near_z, out_z, in_z) if z_first(n, i) else (mid_y, near_y, out_y, in_y)

    def near_copies_of(n, i):
        mid, near, _, _ = buffers(n, i)
        q = slot(n, i)
        return [
            remote(mid.at[q, :, (r + d) % 4], near.at[q, e], zs_sem.at[n, i, e], zr_sem.at[n, i, e], by_z[d])
            for e, d in enumerate((2 if i % 2 == 0 else 14, 1, 15))
        ]

    def near_start(n, i):
        j, q = piece(i), slot(n, i)
        if z_first(n, i):
            core_copy(n, i).wait_recv()
            mid_z[q] = part[n, j, :, :, :, c] + half[n, j]
            if i > 0:
                for copy in near_copies_of(n, i - 1):
                    copy.wait_send()
        else:
            y_copy(n, i).wait_recv()
            mid_y[q] = part[n, j, :, :, y, c] + half[n, j, :, :, y] + y_in[q]
        start(near_copies_of(n, i))

    def out_copy(n, i, d):
        _, _, out, into = buffers(n, i)
        q = slot(n, i)
        return remote(out.at[q, (k + d) % 4], into.at[q, d], ws_sem.at[n, i, d], wr_sem.at[n, i, d], far(d, piece(i)))

    def outs(i):
        return (2, 1, 3) if i == 0 else (2, 1, 3, 0)

    def out_start(n, i):
        mid, near, out, into = buffers(n, i)
        q = slot(n, i)
        for copy in near_copies_of(n, i):
            copy.wait_recv()
        out[q] = mid[q, :, r] + near[q, 0] + near[q, 1] + near[q, 2]
        for d in outs(i):
            out_copy(n, i, d).start()
        if i == 0:
            into[q, 0] = out[q, k]

    def arrived(n, i):
        into, q = buffers(n, i)[3], slot(n, i)
        for d in outs(i):
            out_copy(n, i, d).wait_recv()
        return into[q, 0] + into[q, 1] + into[q, 2] + into[q, 3]

    def source(i):
        return (x + 4 - i) % 4

    cross_copy = remote(sum_z.at[:, 1 - y], cross_in, ts_sem.at[0], tr_sem.at[0], across)

    def drain(n):
        for i in range(PIECES):
            core_copy(n, i).wait_send()
            for d in outs(i):
                out_copy(n, i, d).wait_send()
            if not (z_first(n, i) and i < 2):
                for copy in near_copies_of(n, i):
                    copy.wait_send()
        y_copy(n, 3).wait_send()

    scale(0)
    scaled_start(0)
    scale(1)
    scaled_start(1)
    near_start(0, 0)
    hand_on(0)
    near_start(0, 1)
    hand_on(1)
    near_start(0, 2)
    out_start(0, 0)
    near_start(0, 3)
    out_start(0, 1)

    @pl.when(x > 0)
    def _():
        for u in range(2):
            swap_copy(u).wait_recv()
            for i, g in enumerate((1, 3)):
                @pl.when(x != g)
                def _():
                    act_copy(2 * u + i, 1).wait_recv()
        gram(s8, a4, part.at[1], 0)
        core_copy(1, 0).start()
        core_copy(1, 1).start()
        y_start(1, 0)
        core_copy(1, 2).start()
        core_copy(1, 3).start()

    out_start(0, 2)

    @pl.when(x > 0)
    def _():
        y_start(1, 1)
        near_start(1, 0)

    out_start(0, 3)

    @pl.when(x > 0)
    def _():
        y_start(1, 2)
        near_start(1, 1)
        y_start(1, 3)
        out_start(1, 0)
        near_start(1, 2)
        out_start(1, 1)
        near_start(1, 3)
        out_start(1, 2)
        out_start(1, 3)

    for i in range(3):
        sum_z[i] = arrived(0, i)
    cross_copy.start()
    loc[3].wait()

    def factors(i, total):
        b = source(i)
        nf_out[b] = FACTOR_DECAY * old_v[b] + ((1.0 - FACTOR_DECAY) / TOKENS) * total

    factors(3, arrived(0, 3))
    cross_copy.wait_recv()
    for i in range(3):
        factors(i, sum_z[i, y] + cross_in[i])

    for i in range(PIECES):
        @pl.when(source(i) > 0)
        def _():
            pr_out[source(i) - 1] = arrived(1, i) * (1.0 / TOKENS)

    for copy in inv_copies + x_copies + near_copies + [cross_copy]:
        copy.wait_send()
    for u in range(2):
        for d in (1, 2, 3):
            far_copy(u, d).wait_send()
        for d in range(4):
            for i in range(3):
                adj_copy(u, d, i).wait_send()
        for i in range(6):
            pass_copy(u, i, c).wait_send()
    drain(0)

    @pl.when(x == 0)
    def _():
        for j in range(PIECES):
            act_copy(j, 1).wait_send()
            act_copy(j, 3).wait_send()

    for i, g in enumerate((1, 3)):
        @pl.when(x == g)
        def _():
            for u in range(2):
                hand_copy(2 * u + i).wait_send()

    @pl.when(x > 0)
    def _():
        for u in range(2):
            swap_copy(u).wait_send()
        drain(1)


def body(activations, output_grads, old_factors, inverses, owners):
    vmem = pl.BlockSpec(memory_space=pltpu.VMEM)
    hbm = pl.BlockSpec(memory_space=pl.ANY)
    bf16, f32 = jnp.bfloat16, jnp.float32
    dma = lambda *shape: pltpu.SemaphoreType.DMA(shape)
    new_factors, preconditioned = pl.pallas_call(
        kernel,
        out_shape=(
            jax.ShapeDtypeStruct((4, ROWS, LANE), f32),
            jax.ShapeDtypeStruct((3, ROWS, LANE), f32),
        ),
        in_specs=[hbm, hbm, hbm, hbm, pl.BlockSpec(memory_space=pltpu.SMEM)],
        out_specs=(vmem, vmem),
        scratch_shapes=[
            pltpu.VMEM((4, TOK, LANE), bf16),
            pltpu.VMEM((8, TOK, LANE), bf16),
            pltpu.VMEM((8, ROWS, 512), bf16),
            pltpu.VMEM((2, 4, 4, 2, 2, ROWS, 256), bf16),
            pltpu.VMEM((8, TOK, LANE), bf16),
            pltpu.VMEM((4, TOK, LANE), bf16),
            pltpu.VMEM((4, ROWS, LANE), f32),
            pltpu.VMEM((2, PIECES, 4, 4, 2, 2, ROWS, LANE), f32),
            pltpu.VMEM((2, PIECES, 4, 4, 2, ROWS, LANE), f32),
            pltpu.VMEM((3, 4, 4, 2, ROWS, LANE), f32),
            pltpu.VMEM((3, 3, 4, 2, ROWS, LANE), f32),
            pltpu.VMEM((3, 4, 2, ROWS, LANE), f32),
            pltpu.VMEM((3, 4, 2, ROWS, LANE), f32),
            pltpu.VMEM((3, 2, ROWS, LANE), f32),
            pltpu.VMEM((3, ROWS, LANE), f32),
            pltpu.VMEM((5, 4, 4, ROWS, LANE), f32),
            pltpu.VMEM((5, 4, 4, ROWS, LANE), f32),
            pltpu.VMEM((5, 4, 4, ROWS, LANE), f32),
            pltpu.VMEM((5, 3, 4, ROWS, LANE), f32),
            pltpu.VMEM((5, 4, ROWS, LANE), f32),
            pltpu.VMEM((5, 4, ROWS, LANE), f32),
            dma(4),
            dma(8), dma(8), dma(8), dma(8), dma(3), dma(3), dma(2, 4), dma(2, 4), dma(2, 4, 3), dma(2, 4, 3), dma(2, 6),
            dma(2, 6), dma(2), dma(2), dma(4, 2), dma(4), dma(2, 4), dma(2, 4), dma(5), dma(5),
            dma(2, 4, 3), dma(2, 4, 3), dma(2, 4, 4), dma(2, 4, 4), dma(1), dma(1),
            pltpu.SemaphoreType.REGULAR, pltpu.SemaphoreType.REGULAR,
        ],
        compiler_params=pltpu.CompilerParams(
            collective_id=0, has_side_effects=True, vmem_limit_bytes=60 * 1024 * 1024
        ),
    )(
        jnp.swapaxes(activations, 0, 1),
        jnp.swapaxes(output_grads, 0, 1),
        old_factors,
        inverses.reshape(ROWS, 1024),
        owners,
    )
    return new_factors, preconditioned.reshape(3, ROWS, 1, LANE)


def solution(mesh):
    placed = (
        P("dp", None, "own"),
        P("dp", None, "own"),
        P(None, "dp", "own"),
        P("own", None, "dp", None),
        P(),
    )
    return jax.shard_map(
        body,
        mesh=mesh,
        in_specs=placed,
        out_specs=(P(None, "dp", "own"), P(None, "dp", None, "own")),
        check_vma=False,
    )
```

time: 97 us -> 89.7 us (0.925)
  the two profiles are of different devices: /device:TPU:6 before, /device:TPU:8 now
where the time goes in v4:
time: 89.7 us; the launch traced here: 89.5 us
  Pallas kernels  86.9 us (97%)
  local copies, waits for them, and re-layouts  1.99 us (2%)
    pallas_call x1, Pallas kernels, body(): pl.pallas_call(kernel, out_shape=(jax.ShapeDtypeStruct((4, ROWS, LANE), f...  86.9 us
    unnamed x4, local copies, waits for them, and re-layouts  1.99 us

profile of v4, /device:TPU:8, one launch (start us, length us, event | category | flops | bytes accessed | tf_op | source)
XLA Modules:
  0.0 89.5 jit_solution(13910237776306540018)
XLA Ops:
  0.6 86.9 %shard_map.68 = (f32[4,16,128]{2,1,0:T(8,128)}, f32[3,16,128]{2,1,0:T(8,128)}) custom-call(bf16[1,512,128]{2,1,0:T(8,128)(2,1)} %bitcast.7, bf16[3,512,128]{2,1,0:T(8,128)(2,1)} %bitcast.6, f32[4,16,128]{2,1,0:T(8,128)} %old.1, bf16[16,1024]{1,0:T(8,128)(2,1)} %bitcast.8, s32[4]{0:T(128)} %owners.1), custom_call_target="tpu_custom_call" | custom-call | tf_op jit(solution)/shard_map/pallas_call | solution.py:411
  87.5 0.0 copy-start
  87.5 1.4 %copy.10 = f32[4,16,128]{2,1,0:T(8,128)} copy(f32[4,16,128]{2,1,0:T(8,128)} %get-tuple-element.10) | data formatting | bytes 65536
  88.9 0.0 copy-done
  88.9 0.6 copy.11
Async XLA Ops:
  87.5 1.4 %copy-start = (f32[3,16,128]{2,1,0:T(8,128)S(1)}, f32[3,16,128]{2,1,0:T(8,128)}, u32[]{:S(2)}) copy-start(f32[3,16,128]{2,1,0:T(8,128)} %get-tuple-element.5) | copy-start | bytes 73732

commit v5 on v4

--- a/solution.py
+++ b/solution.py
@@ -14,14 +14,14 @@
 ROWS = 16
 
 
-def gram(lhs8, rhs4, part, j_base):
-    rhs = jnp.concatenate([rhs4[j_base + j] for j in range(PIECES)], axis=1)
+def gram(lhs8, rhs4, part, j_base, pieces):
+    rhs = jnp.concatenate([rhs4[j_base + j] for j in pieces], axis=1)
 
     def tile(i, _):
         lhs = jnp.concatenate([lhs8[2 * i], lhs8[2 * i + 1]], axis=1)
         out = lax.dot_general(lhs, rhs, (((0,), (0,)), ((), ())), preferred_element_type=jnp.float32)
-        for j in range(PIECES):
-            part[j, i] = out[:, j * LANE:(j + 1) * LANE].reshape(4, 2, 2, ROWS, LANE)
+        for e, j in enumerate(pieces):
+            part[j, i] = out[:, e * LANE:(e + 1) * LANE].reshape(4, 2, 2, ROWS, LANE)
         return 0
 
     lax.fori_loop(0, 4, tile, 0)
@@ -29,7 +29,7 @@
 
 def kernel(
     act, grads, old, inv, owners, nf_out, pr_out,
-    cols, x8, shard, full_inv, s8, a4, old_v, part, half,
+    owner_s, cols, x8, shard, full_inv, s8, a4, old_v, part, half,
     mid_z, near_z, out_z, in_z, sum_z, cross_in,
     y_out, y_in, mid_y, near_y, out_y, in_y,
     loc_sem, xs_sem, xr_sem, is_sem, ir_sem, ns_sem, nr_sem, fs_sem, fr_sem, as_sem, ar_sem, ps_sem, pr_sem,
@@ -66,6 +66,7 @@
         pltpu.make_async_copy(grads, cols.at[pl.ds(1, 3)], loc_sem.at[1]),
         pltpu.make_async_copy(inv.at[:, pl.ds(h * 512, 512)], shard.at[own], loc_sem.at[2]),
         pltpu.make_async_copy(old, old_v, loc_sem.at[3]),
+        pltpu.make_async_copy(owners, owner_s, loc_sem.at[4]),
     ]
     for copy in loc:
         copy.start()
@@ -96,10 +97,11 @@
     for d in (1, 3):
         pl.semaphore_signal(chain_4, inc=1, device_id=far(d, x), device_id_type=MESH)
     loc[2].wait()
+    loc[4].wait()
     for copy in inv_copies:
         copy.wait_recv()
 
-    mine = shard[owners[x]]
+    mine = shard[owner_s[x]]
     for u in range(2):
         full_inv[u, k, r, y, c] = mine[:, u * 256:(u + 1) * 256]
     here = full_inv.at[:, k, r, y, c]
@@ -162,7 +164,7 @@
 
     for copy in x_copies:
         copy.wait_recv()
-    gram(x8, x8, part.at[0], h * PIECES)
+    gram(x8, x8, part.at[0], h * PIECES, range(PIECES))
 
     def piece(i):
         return (x + i) % 4
@@ -188,8 +190,8 @@
         j = piece(i)
         core_copy(n, i).wait_recv()
         y_out[slot(n, i)] = part[n, j, :, :, 1 - y, c] + half[n, j, :, :, 1 - y]
-        if n == 1 and i > 0:
-            y_copy(n, i - 1).wait_send()
+        if n == 1 and i > 1:
+            y_copy(n, i - 2).wait_send()
         y_copy(n, i).start()
 
     y_start(0, 3)
@@ -256,9 +258,6 @@
         if z_first(n, i):
             core_copy(n, i).wait_recv()
             mid_z[q] = part[n, j, :, :, :, c] + half[n, j]
-            if i > 0:
-                for copy in near_copies_of(n, i - 1):
-                    copy.wait_send()
         else:
             y_copy(n, i).wait_recv()
             mid_y[q] = part[n, j, :, :, y, c] + half[n, j, :, :, y] + y_in[q]
@@ -299,18 +298,18 @@
             core_copy(n, i).wait_send()
             for d in outs(i):
                 out_copy(n, i, d).wait_send()
-            if not (z_first(n, i) and i < 2):
-                for copy in near_copies_of(n, i):
-                    copy.wait_send()
-        y_copy(n, 3).wait_send()
+            for copy in near_copies_of(n, i):
+                copy.wait_send()
+        for i in range(3 - n, 4):
+            y_copy(n, i).wait_send()
 
     scale(0)
     scaled_start(0)
+    near_start(0, 0)
+    near_start(0, 1)
     scale(1)
     scaled_start(1)
-    near_start(0, 0)
     hand_on(0)
-    near_start(0, 1)
     hand_on(1)
     near_start(0, 2)
     out_start(0, 0)
@@ -325,9 +324,10 @@
                 @pl.when(x != g)
                 def _():
                     act_copy(2 * u + i, 1).wait_recv()
-        gram(s8, a4, part.at[1], 0)
+        gram(s8, a4, part.at[1], 0, [piece(0), piece(1)])
         core_copy(1, 0).start()
         core_copy(1, 1).start()
+        gram(s8, a4, part.at[1], 0, [piece(2), piece(3)])
         y_start(1, 0)
         core_copy(1, 2).start()
         core_copy(1, 3).start()
@@ -414,9 +414,10 @@
             jax.ShapeDtypeStruct((4, ROWS, LANE), f32),
             jax.ShapeDtypeStruct((3, ROWS, LANE), f32),
         ),
-        in_specs=[hbm, hbm, hbm, hbm, pl.BlockSpec(memory_space=pltpu.SMEM)],
+        in_specs=[hbm, hbm, hbm, hbm, hbm],
         out_specs=(vmem, vmem),
         scratch_shapes=[
+            pltpu.SMEM((4,), jnp.int32),
             pltpu.VMEM((4, TOK, LANE), bf16),
             pltpu.VMEM((8, TOK, LANE), bf16),
             pltpu.VMEM((8, ROWS, 512), bf16),
@@ -438,7 +439,7 @@
             pltpu.VMEM((5, 3, 4, ROWS, LANE), f32),
             pltpu.VMEM((5, 4, ROWS, LANE), f32),
             pltpu.VMEM((5, 4, ROWS, LANE), f32),
-            dma(4),
+            dma(5),
             dma(8), dma(8), dma(8), dma(8), dma(3), dma(3), dma(2, 4), dma(2, 4), dma(2, 4, 3), dma(2, 4, 3), dma(2, 6),
             dma(2, 6), dma(2), dma(2), dma(4, 2), dma(4), dma(2, 4), dma(2, 4), dma(5), dma(5),
             dma(2, 4, 3), dma(2, 4, 3), dma(2, 4, 4), dma(2, 4, 4), dma(1), dma(1),

time: 89.7 us -> 88.2 us (0.983)
  the two profiles are of different devices: /device:TPU:8 before, /device:TPU:10 now
where the time goes in v5:
time: 88.2 us; the launch traced here: 88.1 us
  Pallas kernels  85.4 us (97%)
  local copies, waits for them, and re-layouts  1.99 us (2%)
    pallas_call x1, Pallas kernels, body(): pl.pallas_call(kernel, out_shape=(jax.ShapeDtypeStruct((4, ROWS, LANE), f...  85.4 us
    unnamed x4, local copies, waits for them, and re-layouts  1.99 us

profile of v5, /device:TPU:10, one launch (start us, length us, event | category | flops | bytes accessed | tf_op | source)
XLA Modules:
  0.0 88.1 jit_solution(13132182877547400928)
XLA Ops:
  0.6 85.4 %shard_map.68 = (f32[4,16,128]{2,1,0:T(8,128)}, f32[3,16,128]{2,1,0:T(8,128)}) custom-call(bf16[1,512,128]{2,1,0:T(8,128)(2,1)} %bitcast.7, bf16[3,512,128]{2,1,0:T(8,128)(2,1)} %bitcast.6, f32[4,16,128]{2,1,0:T(8,128)} %old.1, bf16[16,1024]{1,0:T(8,128)(2,1)} %bitcast.8, s32[4]{0:T(128)} %owners.1), custom_call_target="tpu_custom_call" | custom-call | tf_op jit(solution)/shard_map/pallas_call | solution.py:411
  86.1 0.0 copy-start
  86.1 1.4 %copy.10 = f32[4,16,128]{2,1,0:T(8,128)} copy(f32[4,16,128]{2,1,0:T(8,128)} %get-tuple-element.10) | data formatting | bytes 65536
  87.4 0.0 copy-done
  87.4 0.6 copy.11
Async XLA Ops:
  86.1 1.4 %copy-start = (f32[3,16,128]{2,1,0:T(8,128)S(1)}, f32[3,16,128]{2,1,0:T(8,128)}, u32[]{:S(2)}) copy-start(f32[3,16,128]{2,1,0:T(8,128)} %get-tuple-element.5) | copy-start | bytes 73732

commit v6 on v5

--- a/solution.py
+++ b/solution.py
@@ -61,6 +61,10 @@
     by_z = {d: at(z + d, y, c, own) for d in (1, 15, 2, 14)}
     peers = [((h + d // 4) % 2, (x + d % 4) % 4) for d in range(8)]
 
+    barrier = pltpu.get_barrier_semaphore()
+    targets = list(by_z.values()) + [member(*peers[d]) for d in range(1, 8)] + [core, across, diagonal]
+    for target in targets:
+        pl.semaphore_signal(barrier, inc=1, device_id=target, device_id_type=MESH)
     loc = [
         pltpu.make_async_copy(act, cols.at[pl.ds(0, 1)], loc_sem.at[0]),
         pltpu.make_async_copy(grads, cols.at[pl.ds(1, 3)], loc_sem.at[1]),
@@ -71,10 +75,6 @@
     for copy in loc:
         copy.start()
 
-    barrier = pltpu.get_barrier_semaphore()
-    targets = list(by_z.values()) + [member(*peers[d]) for d in range(1, 8)] + [core, across, diagonal]
-    for target in targets:
-        pl.semaphore_signal(barrier, inc=1, device_id=target, device_id_type=MESH)
     pl.semaphore_wait(barrier, len(targets))
     for d in (2, 14):
         pl.semaphore_signal(chain_2, inc=1, device_id=by_z[d], device_id_type=MESH)
@@ -190,8 +190,8 @@
         j = piece(i)
         core_copy(n, i).wait_recv()
         y_out[slot(n, i)] = part[n, j, :, :, 1 - y, c] + half[n, j, :, :, 1 - y]
-        if n == 1 and i > 1:
-            y_copy(n, i - 2).wait_send()
+        if n == 1 and i in (3, 0):
+            y_copy(n, 1 if i == 3 else 2).wait_send()
         y_copy(n, i).start()
 
     y_start(0, 3)
@@ -300,7 +300,7 @@
                 out_copy(n, i, d).wait_send()
             for copy in near_copies_of(n, i):
                 copy.wait_send()
-        for i in range(3 - n, 4):
+        for i in (3, 0)[:1 + n]:
             y_copy(n, i).wait_send()
 
     scale(0)
@@ -324,53 +324,39 @@
                 @pl.when(x != g)
                 def _():
                     act_copy(2 * u + i, 1).wait_recv()
-        gram(s8, a4, part.at[1], 0, [piece(0), piece(1)])
+        gram(s8, a4, part.at[1], 0, [piece(1), piece(2)])
+        core_copy(1, 1).start()
+        core_copy(1, 2).start()
+        gram(s8, a4, part.at[1], 0, [piece(3), piece(0)])
+        y_start(1, 1)
+        core_copy(1, 3).start()
         core_copy(1, 0).start()
-        core_copy(1, 1).start()
-        gram(s8, a4, part.at[1], 0, [piece(2), piece(3)])
-        y_start(1, 0)
-        core_copy(1, 2).start()
-        core_copy(1, 3).start()
 
     out_start(0, 2)
-
-    @pl.when(x > 0)
-    def _():
-        y_start(1, 1)
-        near_start(1, 0)
-
-    out_start(0, 3)
 
     @pl.when(x > 0)
     def _():
         y_start(1, 2)
         near_start(1, 1)
+
+    out_start(0, 3)
+
+    @pl.when(x > 0)
+    def _():
         y_start(1, 3)
-        out_start(1, 0)
         near_start(1, 2)
+        y_start(1, 0)
         out_start(1, 1)
         near_start(1, 3)
         out_start(1, 2)
+        near_start(1, 0)
         out_start(1, 3)
+        out_start(1, 0)
 
     for i in range(3):
         sum_z[i] = arrived(0, i)
     cross_copy.start()
     loc[3].wait()
-
-    def factors(i, total):
-        b = source(i)
-        nf_out[b] = FACTOR_DECAY * old_v[b] + ((1.0 - FACTOR_DECAY) / TOKENS) * total
-
-    factors(3, arrived(0, 3))
-    cross_copy.wait_recv()
-    for i in range(3):
-        factors(i, sum_z[i, y] + cross_in[i])
-
-    for i in range(PIECES):
-        @pl.when(source(i) > 0)
-        def _():
-            pr_out[source(i) - 1] = arrived(1, i) * (1.0 / TOKENS)
 
     for copy in inv_copies + x_copies + near_copies + [cross_copy]:
         copy.wait_send()
@@ -401,6 +387,21 @@
         for u in range(2):
             swap_copy(u).wait_send()
         drain(1)
+
+
+    def factors(i, total):
+        b = source(i)
+        nf_out[b] = FACTOR_DECAY * old_v[b] + ((1.0 - FACTOR_DECAY) / TOKENS) * total
+
+    factors(3, arrived(0, 3))
+    cross_copy.wait_recv()
+    for i in range(3):
+        factors(i, sum_z[i, y] + cross_in[i])
+
+    for i in (1, 2, 3, 0):
+        @pl.when(source(i) > 0)
+        def _():
+            pr_out[source(i) - 1] = arrived(1, i) * (1.0 / TOKENS)
 
 
 def body(activations, output_grads, old_factors, inverses, owners):

time: 88.2 us -> 87.5 us (level)
  the two profiles are of different devices: /device:TPU:10 before, /device:TPU:6 now
where the time goes in v6:
time: 87.5 us; the launch traced here: 86.9 us
  Pallas kernels  84.2 us (96%)
  local copies, waits for them, and re-layouts  1.99 us (2%)
    pallas_call x1, Pallas kernels, body(): pl.pallas_call(kernel, out_shape=(jax.ShapeDtypeStruct((4, ROWS, LANE), f...  84.2 us
    unnamed x4, local copies, waits for them, and re-layouts  1.99 us

profile of v6, /device:TPU:6, one launch (start us, length us, event | category | flops | bytes accessed | tf_op | source)
XLA Modules:
  0.0 86.9 jit_solution(16779474681737913823)
XLA Ops:
  0.6 84.2 %shard_map.68 = (f32[4,16,128]{2,1,0:T(8,128)}, f32[3,16,128]{2,1,0:T(8,128)}) custom-call(bf16[1,512,128]{2,1,0:T(8,128)(2,1)} %bitcast.7, bf16[3,512,128]{2,1,0:T(8,128)(2,1)} %bitcast.6, f32[4,16,128]{2,1,0:T(8,128)} %old.1, bf16[16,1024]{1,0:T(8,128)(2,1)} %bitcast.8, s32[4]{0:T(128)} %owners.1), custom_call_target="tpu_custom_call" | custom-call | tf_op jit(solution)/shard_map/pallas_call | solution.py:412
  84.9 0.0 copy-start
  84.9 1.4 %copy.10 = f32[4,16,128]{2,1,0:T(8,128)} copy(f32[4,16,128]{2,1,0:T(8,128)} %get-tuple-element.10) | data formatting | bytes 65536
  86.3 0.0 copy-done
  86.3 0.6 copy.11
Async XLA Ops:
  84.9 1.4 %copy-start = (f32[3,16,128]{2,1,0:T(8,128)S(1)}, f32[3,16,128]{2,1,0:T(8,128)}, u32[]{:S(2)}) copy-start(f32[3,16,128]{2,1,0:T(8,128)} %get-tuple-element.5) | copy-start | bytes 73732

commit v7 on v6

--- a/solution.py
+++ b/solution.py
@@ -28,7 +28,7 @@
 
 
 def kernel(
-    act, grads, old, inv, owners, nf_out, pr_out,
+    act, grads, old, inv, owners, nf_hbm, pr_hbm, nf_out, pr_out,
     owner_s, cols, x8, shard, full_inv, s8, a4, old_v, part, half,
     mid_z, near_z, out_z, in_z, sum_z, cross_in,
     y_out, y_in, mid_y, near_y, out_y, in_y,
@@ -398,14 +398,21 @@
     for i in range(3):
         factors(i, sum_z[i, y] + cross_in[i])
 
+    nf_copy = pltpu.make_async_copy(nf_out, nf_hbm, loc_sem.at[5])
+    nf_copy.start()
+
     for i in (1, 2, 3, 0):
         @pl.when(source(i) > 0)
         def _():
             pr_out[source(i) - 1] = arrived(1, i) * (1.0 / TOKENS)
 
+    pr_copy = pltpu.make_async_copy(pr_out, pr_hbm, loc_sem.at[6])
+    pr_copy.start()
+    nf_copy.wait()
+    pr_copy.wait()
+
 
 def body(activations, output_grads, old_factors, inverses, owners):
-    vmem = pl.BlockSpec(memory_space=pltpu.VMEM)
     hbm = pl.BlockSpec(memory_space=pl.ANY)
     bf16, f32 = jnp.bfloat16, jnp.float32
     dma = lambda *shape: pltpu.SemaphoreType.DMA(shape)
@@ -416,8 +423,10 @@
             jax.ShapeDtypeStruct((3, ROWS, LANE), f32),
         ),
         in_specs=[hbm, hbm, hbm, hbm, hbm],
-        out_specs=(vmem, vmem),
+        out_specs=(hbm, hbm),
         scratch_shapes=[
+            pltpu.VMEM((4, ROWS, LANE), f32),
+            pltpu.VMEM((3, ROWS, LANE), f32),
             pltpu.SMEM((4,), jnp.int32),
             pltpu.VMEM((4, TOK, LANE), bf16),
             pltpu.VMEM((8, TOK, LANE), bf16),
@@ -440,7 +449,7 @@
             pltpu.VMEM((5, 3, 4, ROWS, LANE), f32),
             pltpu.VMEM((5, 4, ROWS, LANE), f32),
             pltpu.VMEM((5, 4, ROWS, LANE), f32),
-            dma(5),
+            dma(7),
             dma(8), dma(8), dma(8), dma(8), dma(3), dma(3), dma(2, 4), dma(2, 4), dma(2, 4, 3), dma(2, 4, 3), dma(2, 6),
             dma(2, 6), dma(2), dma(2), dma(4, 2), dma(4), dma(2, 4), dma(2, 4), dma(5), dma(5),
             dma(2, 4, 3), dma(2, 4, 3), dma(2, 4, 4), dma(2, 4, 4), dma(1), dma(1),

time: 87.5 us -> 87.8 us (level)
  no operation moved by 1% of the time
where the time goes in v7:
time: 87.8 us; the launch traced here: 86.9 us
  Pallas kernels  84.2 us (96%)
  local copies, waits for them, and re-layouts  1.99 us (2%)
    pallas_call x1, Pallas kernels, body(): pl.pallas_call(kernel, out_shape=(jax.ShapeDtypeStruct((4, ROWS, LANE), f...  84.2 us
    unnamed x4, local copies, waits for them, and re-layouts  1.99 us

profile of v7, /device:TPU:6, one launch (start us, length us, event | category | flops | bytes accessed | tf_op | source)
XLA Modules:
  0.0 86.9 jit_solution(3945687416363771552)
XLA Ops:
  0.6 84.2 %shard_map.68 = (f32[4,16,128]{2,1,0:T(8,128)}, f32[3,16,128]{2,1,0:T(8,128)}) custom-call(bf16[1,512,128]{2,1,0:T(8,128)(2,1)} %bitcast.7, bf16[3,512,128]{2,1,0:T(8,128)(2,1)} %bitcast.6, f32[4,16,128]{2,1,0:T(8,128)} %old.1, bf16[16,1024]{1,0:T(8,128)(2,1)} %bitcast.8, s32[4]{0:T(128)} %owners.1), custom_call_target="tpu_custom_call" | custom-call | tf_op jit(solution)/shard_map/pallas_call | solution.py:419
  84.9 0.0 copy-start
  84.9 1.4 %copy.10 = f32[4,16,128]{2,1,0:T(8,128)} copy(f32[4,16,128]{2,1,0:T(8,128)} %get-tuple-element.10) | data formatting | bytes 65536
  86.3 0.0 copy-done
  86.3 0.6 copy.11
Async XLA Ops:
  84.9 1.4 %copy-start = (f32[3,16,128]{2,1,0:T(8,128)S(1)}, f32[3,16,128]{2,1,0:T(8,128)}, u32[]{:S(2)}) copy-start(f32[3,16,128]{2,1,0:T(8,128)} %get-tuple-element.5) | copy-start | bytes 73732
